TPU v7x, 256 devices: a whole 4x4x8 slice. The times are simulated.
256 devices in a mesh: tm: 64 (over y, z, core), chan: 4 (over x).
Axes of the slice: x: 4, y: 4, z: 8, core: 2. Of those that a mesh axis runs over, the one named last changes fastest.
Arguments:
- reference_signal: float32 [2, 131072], P(None, 'tm'), may hold values from -12 to 12, as said below
- surveillance: float32 [2, 64, 131072], P(None, 'chan', 'tm'), may hold values from -30 to 30, as said below
- loading: float32 [1], replicated, may hold values from 0.0005 to 0.005
Outputs:
- range_doppler: float32 [256, 2, 64, 1024], P(('tm', 'chan'))
- clutter_weights: float32 [2, 256, 64], P(None, None, 'chan')
Inputs may be any that keep to these rules, and one draw needn't show every extreme that they name: `reference_signal`: complex reference samples; row 0 holds the real parts, row 1 the imaginary parts. `surveillance`: complex surveillance samples; index 0 of the first dimension holds the real parts, index 1 the imaginary parts.
All inputs are finite; a program needn't handle non-finite values.
Results may differ from a plain program's by a relative error of at most 0.0003.
Values sent between devices are 32-bit elements; how exact they have to be, the bound alone decides.
A program may use at most 64 MiB of HBM per device.

v0:
```python
import functools

import jax
import jax.numpy as jnp
import numpy as np
from jax import lax
from jax.experimental import pallas as pl
from jax.experimental.pallas import tpu as pltpu
from jax.sharding import Mesh
from jax.sharding import PartitionSpec as P

LAGS = 256
DOPP = 1024
SEG_LEN = 512
TM = ("tm_0", "tm_1", "tm_2")
TM_CHAN = ("tm_0", "tm_1", "tm_2", "chan")
EPSILON = 1e-06
PANEL = 32
PIVOTS = 4
ROWS = 40

highest = lax.Precision.HIGHEST
NN = (((1,), (0,)), ((), ()))
NT = (((1,), (1,)), ((), ()))


def dot(a, b, dims=NN):
    return lax.dot_general(a, b, dims, precision=highest, preferred_element_type=jnp.float32)


def halves(x):
    high = x.astype(jnp.bfloat16)
    return high, (x - high.astype(jnp.float32)).astype(jnp.bfloat16)


def dot3(a, b, dims=NN):
    def one(x, y):
        return lax.dot_general(x, y, dims, preferred_element_type=jnp.float32)

    return one(a[0], b[0]) + (one(a[0], b[1]) + one(a[1], b[0]))


def toeplitz(row, rows):
    wide = jnp.broadcast_to(row, (rows, row.shape[1]))
    return pltpu.roll(wide, 0, 1, stride=1, stride_axis=0)


def delays(window):
    tiles = window.shape[1] // 128
    parts = [jnp.zeros((128, 128), jnp.float32)]
    for t in range(1, tiles):
        parts.append(toeplitz(window[:, 128 * t - 128 : 128 * t + 128], 128)[:, 128:])
    return jnp.concatenate(parts, axis=1)


def first_kernel(last_index, position, prior, reference, surveillance, sums, table):
    length = reference.shape[1]
    width = surveillance.shape[1]
    window = jnp.concatenate([prior[...], reference[...]], axis=1)
    taps = []
    for part in range(2):
        taps.append(halves(delays(window[part : part + 1])))
        for piece in range(2):
            table[part, piece] = taps[part][piece]
    s_re, s_im = surveillance[0], surveillance[1]
    r_re, r_im = reference[0:1], reference[1:2]
    blank = jnp.zeros((6, length), jnp.float32)
    with_re = halves(jnp.concatenate([s_re, s_im, r_re, r_im, blank], axis=0))
    with_im = halves(jnp.concatenate([s_im, -s_re, r_im, -r_re, blank], axis=0))
    for half in range(2):
        cut = slice(256 - 128 * half, 256 - 128 * half + length)
        product = dot3([t[:, cut] for t in taps[0]], with_re, NT)
        product = product + dot3([t[:, cut] for t in taps[1]], with_im, NT)
        wide = jnp.concatenate([product, jnp.zeros((128, 128 - ROWS), jnp.float32)], axis=1)
        sums[:, 128 * half : 128 * half + 128] = wide.T[:ROWS]
    owner = jnp.where(position[0] == last_index, 1.0, 0.0)
    sums[34:36, :] = reference[:, length - LAGS :] * owner


def first_pass(prior, reference, surveillance, position, last_index):
    vmem = pl.BlockSpec(memory_space=pltpu.VMEM)
    length = reference.shape[1]
    return pl.pallas_call(
        functools.partial(first_kernel, last_index),
        out_shape=[
            jax.ShapeDtypeStruct((ROWS, LAGS), jnp.float32),
            jax.ShapeDtypeStruct((2, 2, 128, LAGS + length), jnp.bfloat16),
        ],
        in_specs=[pl.BlockSpec(memory_space=pltpu.SMEM), vmem, vmem, vmem],
        out_specs=[vmem, vmem],
        name="first_pass",
    )(position, prior, reference, surveillance)


def times(a, b):
    if a[1] is None and b[1] is None:
        return (a[0] * b[0], None)
    if a[1] is None:
        return (a[0] * b[0], a[0] * b[1])
    if b[1] is None:
        return (a[0] * b[0], a[1] * b[0])
    return (a[0] * b[0] - a[1] * b[1], a[0] * b[1] + a[1] * b[0])


def plus(a, b):
    if a[1] is None:
        return (a[0] + b[0], b[1])
    if b[1] is None:
        return (a[0] + b[0], a[1])
    return (a[0] + b[0], a[1] + b[1])


def minus(a, b):
    return (a[0] - b[0], None if b[1] is None else a[1] - b[1])


def negative(a):
    return (-a[0], None if a[1] is None else -a[1])


def conjugate(a):
    return (a[0], None if a[1] is None else -a[1])


def product(left, right):
    out = []
    for row in left:
        line = []
        for j in range(len(right[0])):
            total = times(row[0], right[0][j])
            for k in range(1, len(row)):
                total = plus(total, times(row[k], right[k][j]))
            line.append(total)
        out.append(line)
    return out


def adjoint(block):
    return [[conjugate(block[j][i]) for j in range(len(block))] for i in range(len(block[0]))]


def hermitian_inverse(block):
    size = len(block)
    if size == 1:
        return [[(1.0 / block[0][0][0], None)]]
    if size == 2:
        a, c, d = block[0][0][0], block[0][1], block[1][1][0]
        scale = 1.0 / (a * d - (c[0] * c[0] + c[1] * c[1]))
        off = (-c[0] * scale, -c[1] * scale)
        return [[(d * scale, None), off], [conjugate(off), (a * scale, None)]]
    half = size // 2
    head = [row[:half] for row in block[:half]]
    side = [row[half:] for row in block[:half]]
    tail = [row[half:] for row in block[half:]]
    head_inverse = hermitian_inverse(head)
    lifted = product(head_inverse, side)
    drop = product(adjoint(side), lifted)
    rest = [[minus(tail[i][j], drop[i][j]) for j in range(half)] for i in range(half)]
    rest_inverse = hermitian_inverse(rest)
    corner = product(lifted, rest_inverse)
    extra = product(corner, adjoint(lifted))
    first = [[plus(head_inverse[i][j], extra[i][j]) for j in range(half)] for i in range(half)]
    right = [[negative(corner[i][j]) for j in range(half)] for i in range(half)]
    below = adjoint(right)
    return [first[i] + right[i] for i in range(half)] + [below[i] + rest_inverse[i] for i in range(half)]


def eliminate(real, imag):
    height, n = real.shape
    m = PIVOTS
    lane = lax.broadcasted_iota(jnp.int32, (1, n), 1)
    lanes = lax.broadcasted_iota(jnp.int32, (height, 128), 1)
    rows = lax.broadcasted_iota(jnp.int32, (height, 128), 0)

    def wide(value):
        return None if value is None else jnp.concatenate([value] * (n // 128), axis=1)

    for k in range(0, height, m):
        col_r = [jnp.broadcast_to(real[:, k + j : k + j + 1], (height, 128)) for j in range(m)]
        col_i = [jnp.broadcast_to(imag[:, k + j : k + j + 1], (height, 128)) for j in range(m)]
        block = [
            [(col_r[j][k + i : k + i + 1], col_i[j][k + i : k + i + 1]) for j in range(m)]
            for i in range(m)
        ]
        inverse = [[(wide(q[0]), wide(q[1])) for q in row] for row in hermitian_inverse(block)]
        hit = (lane >= k) & (lane < k + m)
        old = [
            (
                jnp.where(hit, jnp.where(lane == k + i, 1.0, 0.0), real[k + i : k + i + 1]),
                jnp.where(hit, 0.0, imag[k + i : k + i + 1]),
            )
            for i in range(m)
        ]
        new = product(inverse, [[value] for value in old])
        new = [line[0] for line in new]
        inside = (rows >= k) & (rows < k + m)
        col_r = [jnp.where(inside, jnp.where(rows == k + j, -1.0, 0.0), col_r[j]) for j in range(m)]
        col_i = [jnp.where(inside, 0.0, col_i[j]) for j in range(m)]
        gone = inside | ((lanes >= k) & (lanes < k + m))
        out_r, out_i = [], []
        for t in range(n // 128):
            cut = slice(128 * t, 128 * t + 128)
            mask = gone if t == 0 else inside
            next_r = jnp.where(mask, 0.0, real[:, cut])
            next_i = jnp.where(mask, 0.0, imag[:, cut])
            for j in range(m):
                row_r, row_i = new[j][0][:, cut], new[j][1][:, cut]
                next_r = next_r - (col_r[j] * row_r - col_i[j] * row_i)
                next_i = next_i - (col_r[j] * row_i + col_i[j] * row_r)
            out_r.append(next_r)
            out_i.append(next_i)
        real = jnp.concatenate(out_r, axis=1)
        imag = jnp.concatenate(out_i, axis=1)
    return real, imag


def invert(real, imag):
    b = PANEL

    def panel(index, carry):
        start = pl.multiple_of(index * b, b)
        held = pl.ds(start, b)
        top_r, top_i = eliminate(real[held, :], imag[held, :])
        all_r, all_i = real[...], imag[...]
        lane = lax.broadcasted_iota(jnp.int32, (LAGS, 128), 1)
        row = lax.broadcasted_iota(jnp.int32, (LAGS, 128), 0)
        factor = jnp.where(lane < b, all_r[:, :128], pltpu.roll(all_i[:, :128], b, 1))
        inside = (row >= start) & (row < start + b)
        factor = jnp.where(inside | (lane >= 2 * b), 0.0, factor)
        right = jnp.concatenate(
            [
                jnp.concatenate([top_r, top_i], axis=1),
                jnp.concatenate([-top_i, top_r], axis=1),
                jnp.zeros((128 - 2 * b, 2 * LAGS), jnp.float32),
            ],
            axis=0,
        )
        update = dot(factor, right)
        column = lax.broadcasted_iota(jnp.int32, (LAGS, LAGS), 1)
        all_r = jnp.where(column < b, 0.0, all_r) - update[:, :LAGS]
        all_i = jnp.where(column < b, 0.0, all_i) - update[:, LAGS:]
        real[...] = pltpu.roll(all_r, LAGS - b, 1)
        imag[...] = pltpu.roll(all_i, LAGS - b, 1)
        real[held, :] = pltpu.roll(top_r, LAGS - b, 1)
        imag[held, :] = pltpu.roll(top_i, LAGS - b, 1)
        return carry

    lax.fori_loop(0, LAGS // b, panel, 0)


def normal_matrix(column, loading):
    i0 = lax.broadcasted_iota(jnp.int32, (LAGS, LAGS), 0)
    i1 = lax.broadcasted_iota(jnp.int32, (LAGS, LAGS), 1)
    flip = jnp.where(i0 + i1 == LAGS - 1, 1.0, 0.0)
    behind = pltpu.roll(dot(column, flip), 1, 1)
    lane = lax.broadcasted_iota(jnp.int32, behind.shape, 1)
    behind = jnp.where(lane == 0, 0.0, behind)
    base_r = toeplitz(jnp.concatenate([column[0:1], behind[0:1]], axis=1), LAGS)[:, :LAGS]
    base_i = toeplitz(jnp.concatenate([-column[1:2], behind[1:2]], axis=1), LAGS)[:, :LAGS]
    blank = jnp.zeros((1, LAGS), jnp.float32)
    edge_r = toeplitz(jnp.concatenate([blank, column[2:3]], axis=1), LAGS)[:, :LAGS]
    edge_i = toeplitz(jnp.concatenate([blank, column[3:4]], axis=1), LAGS)[:, :LAGS]
    one = jnp.concatenate([edge_r, edge_i], axis=1)
    two = jnp.concatenate([edge_i, -edge_r], axis=1)
    real = base_r - dot(one, one, NT)
    imag = base_i - dot(one, two, NT)
    diagonal = i0 == i1
    lam = loading * (jnp.sum(jnp.where(diagonal, real, 0.0)) / LAGS)
    return jnp.where(diagonal, real + lam, real), imag


def solve_kernel(loading, sums, weights, real, imag):
    start_r, start_i = normal_matrix(sums[32:40, :], loading[0])
    real[...] = start_r
    imag[...] = start_i
    invert(real, imag)
    half = (ROWS - 8) // 2
    c_re, c_im = sums[:half, :], sums[half : 2 * half, :]
    weights[...] = dot(sums[: 2 * half, :], real[...], NT) + dot(
        jnp.concatenate([-c_im, c_re], axis=0), imag[...], NT
    )


def solve(sums, loading):
    vmem = pl.BlockSpec(memory_space=pltpu.VMEM)
    return pl.pallas_call(
        solve_kernel,
        out_shape=jax.ShapeDtypeStruct((ROWS - 8, LAGS), jnp.float32),
        in_specs=[pl.BlockSpec(memory_space=pltpu.SMEM), vmem],
        out_specs=vmem,
        scratch_shapes=[pltpu.VMEM((LAGS, LAGS), jnp.float32)] * 2,
        name="solve",
    )(loading, sums)


def second_kernel(weights, table, surveillance, corr, energy):
    length = surveillance.shape[2]
    width = surveillance.shape[1]
    w = weights[...]
    w_re, w_im = w[:width], w[width:]
    on_re = halves(w)
    on_im = halves(jnp.concatenate([-w_im, w_re], axis=0))
    clutter = jnp.zeros((2 * width, length), jnp.float32)
    taps = []
    for half in range(2):
        cut = slice(256 - 128 * half, 256 - 128 * half + length)
        lags = slice(128 * half, 128 * half + 128)
        taps.append([[table[part, piece, :, cut] for piece in range(2)] for part in range(2)])
        clutter = clutter + dot3([x[:, lags] for x in on_re], taps[half][0])
        clutter = clutter + dot3([x[:, lags] for x in on_im], taps[half][1])
    residual = jnp.concatenate([surveillance[0], surveillance[1]], axis=0) - clutter
    energy[...] = jnp.broadcast_to(
        jnp.sum(residual * residual, axis=1, keepdims=True), (2 * width, 128)
    )
    turned = jnp.concatenate([residual[width:], -residual[:width]], axis=0)
    segments = length // SEG_LEN
    row = lax.broadcasted_iota(jnp.int32, (2 * width * segments, length), 0)
    col = lax.broadcasted_iota(jnp.int32, (2 * width * segments, length), 1)
    own = row // (2 * width) == col // SEG_LEN
    with_re = halves(jnp.where(own, jnp.concatenate([residual] * segments, axis=0), 0.0))
    with_im = halves(jnp.where(own, jnp.concatenate([turned] * segments, axis=0), 0.0))
    for half in range(2):
        lags = slice(128 * half, 128 * half + 128)
        corr[lags, :] = dot3(taps[half][0], with_re, NT) + dot3(taps[half][1], with_im, NT)


def second_pass(weights, table, surveillance):
    vmem = pl.BlockSpec(memory_space=pltpu.VMEM)
    width, length = surveillance.shape[1:]
    return pl.pallas_call(
        second_kernel,
        out_shape=[
            jax.ShapeDtypeStruct((LAGS, 2 * width * (length // SEG_LEN)), jnp.float32),
            jax.ShapeDtypeStruct((2 * width, 128), jnp.float32),
        ],
        in_specs=[vmem] * 3,
        out_specs=[vmem] * 2,
        name="second_pass",
    )(weights, table, surveillance)


def doppler_tables(shards, segments):
    short = DOPP // segments
    angle = 2.0 * np.pi / short * (np.outer(np.arange(shards), np.arange(short)) % short)
    table = np.concatenate([np.cos(angle), np.sin(angle)], axis=1)
    turn = 2.0 * np.pi / DOPP * np.outer(np.arange(segments), np.arange(DOPP))
    turns = np.stack([np.cos(turn), np.sin(turn)])
    return table.astype(np.float32), turns.astype(np.float32)


def doppler_kernel(cells, scale, table, turns, out):
    shards, groups, lanes = cells.shape
    segments = turns.shape[1]
    width = lanes // segments // 2
    basis = halves(table[...])
    short = DOPP // segments
    for g in range(groups):
        block = halves(cells[:, g, :].T)
        wave = dot3(block, basis)
        total_r = total_i = None
        for s in range(segments):
            base = 2 * width * s
            a_r, a_i = wave[base : base + width, :short], wave[base : base + width, short:]
            b_r, b_i = (
                wave[base + width : base + 2 * width, :short],
                wave[base + width : base + 2 * width, short:],
            )
            y_r = a_r + b_i
            y_i = b_r - a_i
            y_r = jnp.concatenate([y_r] * segments, axis=1)
            y_i = jnp.concatenate([y_i] * segments, axis=1)
            if s == 0:
                total_r, total_i = y_r, y_i
                continue
            c, d = turns[0, s : s + 1, :], turns[1, s : s + 1, :]
            total_r = total_r + (y_r * c + y_i * d)
            total_i = total_i + (y_i * c - y_r * d)
        at = slice(width * g, width * g + width)
        by = scale[at, 0:1]
        out[0, 0, at, :] = total_r * by
        out[0, 1, at, :] = total_i * by


def doppler(cells, scale, segments):
    vmem = pl.BlockSpec(memory_space=pltpu.VMEM)
    table, turns = doppler_tables(cells.shape[0], segments)
    width = cells.shape[2] // segments // 2
    return pl.pallas_call(
        doppler_kernel,
        out_shape=jax.ShapeDtypeStruct((1, 2, width * cells.shape[1], DOPP), jnp.float32),
        in_specs=[vmem] * 4,
        out_specs=vmem,
        name="doppler",
    )(cells, scale, jnp.asarray(table), jnp.asarray(turns))


def per_device(reference_signal, surveillance, loading):
    shards = lax.axis_size(TM)
    length = reference_signal.shape[1]
    width = surveillance.shape[1]
    total = length * shards
    segments = length // SEG_LEN
    here = lax.axis_index(TM)
    pairs = [(i, i + 1) for i in range(shards - 1)]
    prior = lax.ppermute(reference_signal[:, length - LAGS :], TM, pairs)
    local, table = first_pass(prior, reference_signal, surveillance, here[None], shards - 1)
    sums = lax.psum(local, TM)
    weights = solve(sums, loading)
    corr, energy = second_pass(weights, table, surveillance)
    power = lax.psum(energy[:width, 0] + energy[width:, 0], TM)
    scale = lax.rsqrt(total * (power / total + EPSILON))
    scale = lax.all_gather(scale, "chan", tiled=True)
    cells = lax.all_to_all(corr[:, None, :], TM_CHAN, split_axis=0, concat_axis=0, tiled=True)
    cells = cells.reshape(shards, LAGS // shards, corr.shape[1])
    full = doppler(cells, jnp.broadcast_to(scale[:, None], (scale.shape[0], 128)), segments)
    return full, jnp.swapaxes(weights.reshape(2, width, LAGS), 1, 2)


def solution(mesh):
    split = Mesh(
        mesh.devices.reshape(4, 8, 2, mesh.shape["chan"]), ("tm_0", "tm_1", "tm_2", "chan")
    )
    in_specs = (P(None, TM), P(None, "chan", TM), P())
    out_specs = (P(TM_CHAN, None, None, None), P(None, None, "chan"))
    return jax.shard_map(
        per_device, mesh=split, in_specs=in_specs, out_specs=out_specs, check_vma=False
    )
```

profile of v0, /device:TPU:1, one launch (start us, length us, event | category | flops | bytes accessed | tf_op | source)
XLA Modules:
  0.0 434.2 jit_solution(4867955721935000174)
XLA Ops:
  0.6 0.7 slice.9
  1.3 4.9 %collective-permute-start = (f32[2,256]{1,0:T(2,128)S(1)}, f32[2,256]{1,0:T(2,128)S(1)}, u32[]{:S(2)}, u32[]{:S(2)}) collective-permute-start(f32[2,256]{1,0:T(2,128)S(1)} %slice.9), channel_id=1, source_target_pairs={{0,4},{4,8},{8,12},{12,16},{16,20},{20,24},{24,28},{28,32},{32,36}... | collective-permute-start | bytes 6152 | tf_op jit(solution)/shard_map/ppermute | solution.py:405
  6.9 1.3 dynamic-slice
  8.2 0.0 collective-permute-done.prior
  8.2 0.0 copy-start.1
  8.2 0.6 copy-done.1
  8.8 3.5 first_pass.1
  12.3 246.1 %psum.14.sums = f32[40,256]{1,0:T(8,128)} all-reduce(f32[40,256]{1,0:T(8,128)} %get-tuple-element.6), channel_id=1, replica_groups=mesh['tm_0'=4,'tm_1'=8,'tm_2'=2,'chan'=4] {'tm_0','tm_1','tm_2'}, use_global_device_ids=true, to_apply=%region_0.0 | all-reduce | flops 10240 | bytes 81920 | tf_op jit(solution)/shard_map/psum | solution.py:407
  258.4 21.0 %solve.1.weights = f32[32,256]{1,0:T(8,128)} custom-call(f32[1]{0:T(128)S(6)} %copy.9.loading, f32[40,256]{1,0:T(8,128)} %psum.14.sums), custom_call_target="tpu_custom_call" | custom-call | tf_op jit(solution)/shard_map/solve/pallas_call | solution.py:286
  279.4 5.0 %second_pass.1 = (f32[256,128]{1,0:T(8,128)}, f32[32,128]{1,0:T(8,128)}) custom-call(f32[32,256]{1,0:T(8,128)} %solve.1.weights, bf16[2,2,128,2304]{3,2,1,0:T(8,128)(2,1)} %get-tuple-element.7.table, f32[2,16,2048]{2,1,0:T(8,128)} %surveillance.3), custom_call_target="tpu_custom_call" | custom-call | tf_op jit(solution)/shard_map/second_pass/pallas_call | solution.py:330
  284.4 10.7 %all-to-all-start = ((f32[256,1,128]{2,1,0:T(1,128)}), f32[256,1,128]{2,1,0:T(1,128)S(1)}, u32[]{:S(2)}, u32[]{:S(2)}) async-start(f32[256,1,128]{2,1,0:T(1,128)} %bitcast.10), calls=%async_computation | async-start | bytes 262144 | tf_op jit(solution)/shard_map/all_to_all | solution.py:413
  295.1 0.8 add_reduce_fusion
  296.5 125.9 %psum.15 = f32[16]{0:T(128)S(1)} all-reduce(f32[16]{0:T(128)S(1)} %add_reduce_fusion), channel_id=1, replica_groups=mesh['tm_0'=4,'tm_1'=8,'tm_2'=2,'chan'=4] {'tm_0','tm_1','tm_2'}, use_global_device_ids=true, to_apply=%region_1.0 | all-reduce | flops 16 | bytes 128 | tf_op jit(solution)/shard_map/psum | solution.py:410
  422.4 0.1 rsqrt_dynamic-update-slice_fusion
  422.5 8.4 %all-reduce = f32[64]{0:T(128)S(1)} all-reduce(f32[64]{0:T(128)S(1)} %rsqrt_dynamic-update-slice_fusion), channel_id=1, replica_groups=mesh['tm_0'=4,'tm_1'=8,'tm_2'=2,'chan'=4] {'chan'}, use_global_device_ids=true, to_apply=%add | all-reduce | flops 64 | bytes 512
  430.9 0.0 all-to-all-done
  430.9 0.0 copy-start
  430.9 0.7 broadcast_in_dim.14.scale
  431.6 0.0 copy-done
  431.6 2.6 doppler.1
  (1 shorter events, 0.0 us)
Async XLA Ops:
  1.3 6.9 %collective-permute-start = (f32[2,256]{1,0:T(2,128)S(1)}, f32[2,256]{1,0:T(2,128)S(1)}, u32[]{:S(2)}, u32[]{:S(2)}) collective-permute-start(f32[2,256]{1,0:T(2,128)S(1)} %slice.9), channel_id=1, source_target_pairs={{0,4},{4,8},{8,12},{12,16},{16,20},{20,24},{24,28},{28,32},{32,36}... | collective-permute-start | bytes 6152 | tf_op jit(solution)/shard_map/ppermute | solution.py:405
  8.2 0.6 copy-start.1
  284.4 146.5 %all-to-all-start = ((f32[256,1,128]{2,1,0:T(1,128)}), f32[256,1,128]{2,1,0:T(1,128)S(1)}, u32[]{:S(2)}, u32[]{:S(2)}) async-start(f32[256,1,128]{2,1,0:T(1,128)} %bitcast.10), calls=%async_computation | async-start | bytes 262144 | tf_op jit(solution)/shard_map/all_to_all | solution.py:413
  430.9 0.7 copy-start
where the time goes:
time: 439 us; the launch traced here: 434 us
  blocking collectives  380 us (87%)
  Pallas kernels  32.1 us (7%)
  starting transfers between devices  15.6 us (4%)
    psum x1, blocking collectives, per_device(): sums = lax.psum(local, TM)  246 us
    psum x1, blocking collectives, per_device(): power = lax.psum(energy[:width, 0] + energy[width:, 0], TM)  126 us
    pallas_call x1, Pallas kernels, solve(): pl.pallas_call(solve_kernel, out_shape=jax.ShapeDtypeStruct((ROWS - 8, LA...  21 us
    all_to_all x1, starting transfers between devices, per_device(): lax.all_to_all(corr[:, None, :], TM_CHAN, split_axis=0, concat_axis=0, ti...  10.7 us
  transfers between devices with their start and end apart: 2, of which 0 were waited for; matrix products, arithmetic and copies ran while one was open for 1% of the time, Pallas kernels for 0%

commit v1 on v0

--- a/solution.py
+++ b/solution.py
@@ -18,6 +18,7 @@
 PANEL = 32
 PIVOTS = 4
 ROWS = 40
+MESH = pl.DeviceIdType.MESH
 
 highest = lax.Precision.HIGHEST
 NN = (((1,), (0,)), ((), ()))
@@ -45,51 +46,148 @@
     return pltpu.roll(wide, 0, 1, stride=1, stride_axis=0)
 
 
-def delays(window):
-    tiles = window.shape[1] // 128
-    parts = [jnp.zeros((128, 128), jnp.float32)]
-    for t in range(1, tiles):
-        parts.append(toeplitz(window[:, 128 * t - 128 : 128 * t + 128], 128)[:, 128:])
-    return jnp.concatenate(parts, axis=1)
-
-
-def first_kernel(last_index, position, prior, reference, surveillance, sums, table):
+def exchange(axes, src, dst, send, recv):
+    sizes = [lax.axis_size(a) for a in axes]
+    count = int(np.prod(sizes))
+    here = place(axes)
+    copies = []
+    for d in range(1, count):
+        there = lax.rem(here + d, count)
+        copies.append(
+            pltpu.make_async_remote_copy(
+                src_ref=src(there),
+                dst_ref=dst(here),
+                send_sem=send.at[d - 1],
+                recv_sem=recv.at[d - 1],
+                device_id=device(axes, there),
+                device_id_type=MESH,
+            )
+        )
+        copies[-1].start()
+    return copies
+
+
+def place(axes):
+    index = lax.axis_index(axes[0])
+    for a in axes[1:]:
+        index = index * lax.axis_size(a) + lax.axis_index(a)
+    return index
+
+
+def device(axes, index):
+    coordinates = {}
+    for a in reversed(axes):
+        coordinates[a] = lax.rem(index, lax.axis_size(a))
+        index = lax.div(index, lax.axis_size(a))
+    return coordinates
+
+
+def greet(groups):
+    barrier = pltpu.get_barrier_semaphore()
+    total = 0
+    for axes, offsets in groups:
+        count = int(np.prod([lax.axis_size(a) for a in axes]))
+        here = place(axes)
+        for d in offsets:
+            pl.semaphore_signal(
+                barrier, inc=1, device_id=device(axes, lax.rem(here + d, count)), device_id_type=MESH
+            )
+            total += 1
+    return barrier, total
+
+
+def finish(copies):
+    for copy in copies:
+        copy.wait()
+
+
+def first_kernel(
+    reference, surveillance, sums, table,
+    halo, mine, pair, ring_y, ring_z, edge_sem, core_send, core_recv, y_send, y_recv, z_send, z_recv, out_send, out_recv,
+):
     length = reference.shape[1]
-    width = surveillance.shape[1]
-    window = jnp.concatenate([prior[...], reference[...]], axis=1)
-    taps = []
+    count = lax.axis_size(TM)
+    here = place(TM)
+    core, y, z = lax.axis_index(TM[2]), lax.axis_index(TM[0]), lax.axis_index(TM[1])
+    barrier, total = greet(
+        [(TM, (1, count - 1)), (TM[2:], (1,)), (TM[:1], (1, 2, 3)), (TM[1:2], tuple(range(1, 8)))]
+    )
+    pl.semaphore_wait(barrier, total)
+    forward = pltpu.make_async_remote_copy(
+        src_ref=reference.at[:, pl.ds(length - LAGS, LAGS)],
+        dst_ref=halo,
+        send_sem=edge_sem.at[0],
+        recv_sem=edge_sem.at[1],
+        device_id=device(TM, lax.rem(here + 1, count)),
+        device_id_type=MESH,
+    )
+    forward.start()
+
+    def fill(tile, part, window):
+        high, low = halves(toeplitz(window, 128)[:, 128:])
+        cut = slice(128 * tile, 128 * tile + 128)
+        table[part, 0, :, cut] = high
+        table[part, 1, :, cut] = low
+
     for part in range(2):
-        taps.append(halves(delays(window[part : part + 1])))
-        for piece in range(2):
-            table[part, piece] = taps[part][piece]
+        for tile in range(3, (LAGS + length) // 128):
+            fill(tile, part, reference[part : part + 1, 128 * tile - 384 : 128 * tile - 128])
     s_re, s_im = surveillance[0], surveillance[1]
     r_re, r_im = reference[0:1], reference[1:2]
     blank = jnp.zeros((6, length), jnp.float32)
     with_re = halves(jnp.concatenate([s_re, s_im, r_re, r_im, blank], axis=0))
     with_im = halves(jnp.concatenate([s_im, -s_re, r_im, -r_re, blank], axis=0))
+    forward.wait()
+    before = jnp.where(here > 0, halo[...], 0.0)
+    for part in range(2):
+        fill(1, part, before[part : part + 1])
+        fill(2, part, jnp.concatenate([before[part : part + 1, 128:], reference[part : part + 1, :128]], axis=1))
+    owner = jnp.where(here == count - 1, 1.0, 0.0)
     for half in range(2):
         cut = slice(256 - 128 * half, 256 - 128 * half + length)
-        product = dot3([t[:, cut] for t in taps[0]], with_re, NT)
-        product = product + dot3([t[:, cut] for t in taps[1]], with_im, NT)
+        taps = [[table[part, piece, :, cut] for piece in range(2)] for part in range(2)]
+        product = dot3(taps[0], with_re, NT) + dot3(taps[1], with_im, NT)
         wide = jnp.concatenate([product, jnp.zeros((128, 128 - ROWS), jnp.float32)], axis=1)
-        sums[:, 128 * half : 128 * half + 128] = wide.T[:ROWS]
-    owner = jnp.where(position[0] == last_index, 1.0, 0.0)
-    sums[34:36, :] = reference[:, length - LAGS :] * owner
-
-
-def first_pass(prior, reference, surveillance, position, last_index):
+        mine[half] = wide.T[:ROWS]
+        at = length - LAGS + 128 * half
+        mine[half, 34:36, :] = reference[:, at : at + 128] * owner
+
+    finish(exchange(TM[2:], lambda p: mine.at[p], lambda p: pair, core_send, core_recv))
+    ring_y[y] = mine[core] + pair[...]
+    finish(exchange(TM[:1], lambda p: ring_y.at[y], lambda p: ring_y.at[p], y_send, y_recv))
+    ring_z[z] = (ring_y[0] + ring_y[1]) + (ring_y[2] + ring_y[3])
+    finish(exchange(TM[1:2], lambda p: ring_z.at[z], lambda p: ring_z.at[p], z_send, z_recv))
+    sums[core] = ((ring_z[0] + ring_z[1]) + (ring_z[2] + ring_z[3])) + (
+        (ring_z[4] + ring_z[5]) + (ring_z[6] + ring_z[7])
+    )
+    finish(exchange(TM[2:], lambda p: sums.at[core], lambda p: sums.at[p], out_send, out_recv))
+
+
+def first_pass(reference, surveillance):
     vmem = pl.BlockSpec(memory_space=pltpu.VMEM)
     length = reference.shape[1]
+    part = (ROWS, 128)
+    dma = pltpu.SemaphoreType.DMA
     return pl.pallas_call(
-        functools.partial(first_kernel, last_index),
+        first_kernel,
         out_shape=[
-            jax.ShapeDtypeStruct((ROWS, LAGS), jnp.float32),
+            jax.ShapeDtypeStruct((2,) + part, jnp.float32),
             jax.ShapeDtypeStruct((2, 2, 128, LAGS + length), jnp.bfloat16),
         ],
-        in_specs=[pl.BlockSpec(memory_space=pltpu.SMEM), vmem, vmem, vmem],
+        in_specs=[vmem, vmem],
         out_specs=[vmem, vmem],
+        scratch_shapes=[
+            pltpu.VMEM((2, LAGS), jnp.float32),
+            pltpu.VMEM((2,) + part, jnp.float32),
+            pltpu.VMEM(part, jnp.float32),
+            pltpu.VMEM((4,) + part, jnp.float32),
+            pltpu.VMEM((8,) + part, jnp.float32),
+            dma((2,)),
+            dma((1,)), dma((1,)), dma((3,)), dma((3,)), dma((7,)), dma((7,)), dma((1,)), dma((1,)),
+        ],
+        compiler_params=pltpu.CompilerParams(collective_id=0, has_side_effects=True),
         name="first_pass",
-    )(position, prior, reference, surveillance)
+    )(reference, surveillance)
 
 
 def times(a, b):
@@ -270,13 +368,14 @@
 
 
 def solve_kernel(loading, sums, weights, real, imag):
-    start_r, start_i = normal_matrix(sums[32:40, :], loading[0])
+    joined = jnp.concatenate([sums[0], sums[1]], axis=1)
+    start_r, start_i = normal_matrix(joined[32:40, :], loading[0])
     real[...] = start_r
     imag[...] = start_i
     invert(real, imag)
     half = (ROWS - 8) // 2
-    c_re, c_im = sums[:half, :], sums[half : 2 * half, :]
-    weights[...] = dot(sums[: 2 * half, :], real[...], NT) + dot(
+    c_re, c_im = joined[:half, :], joined[half : 2 * half, :]
+    weights[...] = dot(joined[: 2 * half, :], real[...], NT) + dot(
         jnp.concatenate([-c_im, c_re], axis=0), imag[...], NT
     )
 
@@ -293,9 +392,17 @@
     )(loading, sums)
 
 
-def second_kernel(weights, table, surveillance, corr, energy):
+def second_kernel(
+    weights, table, surveillance, cells, energies,
+    corr, landed, turned, power, ring_z, ring_y,
+    far_send, far_recv, near_send, near_recv, z_send, z_recv, y_send, y_recv, e_send, e_recv,
+):
     length = surveillance.shape[2]
     width = surveillance.shape[1]
+    far, near = TM[:2], (TM[2], "chan")
+    z, y, me_far, me_near = place(TM[1:2]), place(TM[:1]), place(far), place(near)
+    barrier, total = greet([(far, tuple(range(1, 32))), (near, tuple(range(1, 8))), (TM[1:2], tuple(range(1, 8))), (TM[:1], (1, 2, 3))])
+    pl.semaphore_wait(barrier, total)
     w = weights[...]
     w_re, w_im = w[:width], w[width:]
     on_re = halves(w)
@@ -309,54 +416,90 @@
         clutter = clutter + dot3([x[:, lags] for x in on_re], taps[half][0])
         clutter = clutter + dot3([x[:, lags] for x in on_im], taps[half][1])
     residual = jnp.concatenate([surveillance[0], surveillance[1]], axis=0) - clutter
-    energy[...] = jnp.broadcast_to(
-        jnp.sum(residual * residual, axis=1, keepdims=True), (2 * width, 128)
-    )
-    turned = jnp.concatenate([residual[width:], -residual[:width]], axis=0)
+    energy = jnp.sum(residual * residual, axis=1, keepdims=True)
+    energy = jnp.broadcast_to(energy[:width] + energy[width:], (width, 128))
+    energy = jnp.concatenate([energy, jnp.zeros((128 - width, 128), jnp.float32)], axis=0)
+    ring_z[z] = energy.T[:8]
+    along_z = exchange(TM[1:2], lambda p: ring_z.at[z], lambda p: ring_z.at[p], z_send, z_recv)
+    swapped = jnp.concatenate([residual[width:], -residual[:width]], axis=0)
     segments = length // SEG_LEN
     row = lax.broadcasted_iota(jnp.int32, (2 * width * segments, length), 0)
     col = lax.broadcasted_iota(jnp.int32, (2 * width * segments, length), 1)
     own = row // (2 * width) == col // SEG_LEN
     with_re = halves(jnp.where(own, jnp.concatenate([residual] * segments, axis=0), 0.0))
-    with_im = halves(jnp.where(own, jnp.concatenate([turned] * segments, axis=0), 0.0))
+    with_im = halves(jnp.where(own, jnp.concatenate([swapped] * segments, axis=0), 0.0))
     for half in range(2):
-        lags = slice(128 * half, 128 * half + 128)
-        corr[lags, :] = dot3(taps[half][0], with_re, NT) + dot3(taps[half][1], with_im, NT)
+        block = dot3(taps[half][0], with_re, NT) + dot3(taps[half][1], with_im, NT)
+        corr[16 * half : 16 * half + 16] = block.reshape(16, 8, 128)
+    to_far = exchange(far, lambda p: corr.at[p], lambda p: landed.at[p], far_send, far_recv)
+    landed[me_far] = corr[me_far]
+    finish(along_z)
+    parts = [ring_z[i] for i in range(8)]
+    ring_y[y] = ((parts[0] + parts[1]) + (parts[2] + parts[3])) + ((parts[4] + parts[5]) + (parts[6] + parts[7]))
+    along_y = exchange(TM[:1], lambda p: ring_y.at[y], lambda p: ring_y.at[p], y_send, y_recv)
+    finish(along_y)
+    power[...] = (ring_y[0] + ring_y[1]) + (ring_y[2] + ring_y[3])
+    energies[me_near] = power[...]
+    to_all = exchange(near, lambda p: power, lambda p: energies.at[p], e_send, e_recv)
+    finish(to_far)
+    everything = landed[...]
+    for lag in range(8):
+        turned[lag] = everything[:, lag, :]
+    to_near = exchange(near, lambda p: turned.at[p], lambda p: cells.at[p], near_send, near_recv)
+    cells[me_near] = turned[me_near]
+    finish(to_all)
+    finish(to_near)
 
 
 def second_pass(weights, table, surveillance):
     vmem = pl.BlockSpec(memory_space=pltpu.VMEM)
-    width, length = surveillance.shape[1:]
+    dma = pltpu.SemaphoreType.DMA
+    f32 = jnp.float32
     return pl.pallas_call(
         second_kernel,
         out_shape=[
-            jax.ShapeDtypeStruct((LAGS, 2 * width * (length // SEG_LEN)), jnp.float32),
-            jax.ShapeDtypeStruct((2 * width, 128), jnp.float32),
+            jax.ShapeDtypeStruct((8, 32, 128), f32),
+            jax.ShapeDtypeStruct((8, 8, 128), f32),
         ],
         in_specs=[vmem] * 3,
         out_specs=[vmem] * 2,
+        scratch_shapes=[
+            pltpu.VMEM((32, 8, 128), f32),
+            pltpu.VMEM((32, 8, 128), f32),
+            pltpu.VMEM((8, 32, 128), f32),
+            pltpu.VMEM((8, 128), f32),
+            pltpu.VMEM((8, 8, 128), f32),
+            pltpu.VMEM((4, 8, 128), f32),
+            dma((31,)), dma((31,)), dma((7,)), dma((7,)), dma((7,)), dma((7,)), dma((3,)), dma((3,)), dma((7,)), dma((7,)),
+        ],
+        compiler_params=pltpu.CompilerParams(collective_id=1, has_side_effects=True),
         name="second_pass",
     )(weights, table, surveillance)
 
 
 def doppler_tables(shards, segments):
     short = DOPP // segments
-    angle = 2.0 * np.pi / short * (np.outer(np.arange(shards), np.arange(short)) % short)
+    order = np.arange(shards).reshape(-1, 2).T.reshape(-1)
+    angle = 2.0 * np.pi / short * (np.outer(order, np.arange(short)) % short)
     table = np.concatenate([np.cos(angle), np.sin(angle)], axis=1)
     turn = 2.0 * np.pi / DOPP * np.outer(np.arange(segments), np.arange(DOPP))
     turns = np.stack([np.cos(turn), np.sin(turn)])
     return table.astype(np.float32), turns.astype(np.float32)
 
 
-def doppler_kernel(cells, scale, table, turns, out):
-    shards, groups, lanes = cells.shape
+def doppler_kernel(samples, cells, energies, table, turns, out):
+    near, _, lanes = cells.shape
+    groups = near // 2
     segments = turns.shape[1]
     width = lanes // segments // 2
     basis = halves(table[...])
     short = DOPP // segments
     for g in range(groups):
-        block = halves(cells[:, g, :].T)
-        wave = dot3(block, basis)
+        power = (energies[g] + energies[groups + g]) / samples
+        scale = lax.rsqrt(samples * (power + EPSILON))
+        by = jnp.broadcast_to(scale[0:1], (128, 128)).T[:width, 0:1]
+        rows = jnp.concatenate([cells[g], cells[groups + g]], axis=0)
+        wave = dot3(halves(rows.T), basis)
         total_r = total_i = None
         for s in range(segments):
             base = 2 * width * s
@@ -365,8 +508,8 @@
                 wave[base + width : base + 2 * width, :short],
                 wave[base + width : base + 2 * width, short:],
             )
-            y_r = a_r + b_i
-            y_i = b_r - a_i
+            y_r = (a_r + b_i) * by
+            y_i = (b_r - a_i) * by
             y_r = jnp.concatenate([y_r] * segments, axis=1)
             y_i = jnp.concatenate([y_i] * segments, axis=1)
             if s == 0:
@@ -376,43 +519,32 @@
             total_r = total_r + (y_r * c + y_i * d)
             total_i = total_i + (y_i * c - y_r * d)
         at = slice(width * g, width * g + width)
-        by = scale[at, 0:1]
-        out[0, 0, at, :] = total_r * by
-        out[0, 1, at, :] = total_i * by
-
-
-def doppler(cells, scale, segments):
+        out[0, 0, at, :] = total_r
+        out[0, 1, at, :] = total_i
+
+
+def doppler(cells, energies, segments, samples):
     vmem = pl.BlockSpec(memory_space=pltpu.VMEM)
-    table, turns = doppler_tables(cells.shape[0], segments)
+    shards = 2 * cells.shape[1]
+    table, turns = doppler_tables(shards, segments)
     width = cells.shape[2] // segments // 2
     return pl.pallas_call(
-        doppler_kernel,
-        out_shape=jax.ShapeDtypeStruct((1, 2, width * cells.shape[1], DOPP), jnp.float32),
+        functools.partial(doppler_kernel, samples),
+        out_shape=jax.ShapeDtypeStruct((1, 2, width * cells.shape[0] // 2, DOPP), jnp.float32),
         in_specs=[vmem] * 4,
         out_specs=vmem,
         name="doppler",
-    )(cells, scale, jnp.asarray(table), jnp.asarray(turns))
+    )(cells, energies, jnp.asarray(table), jnp.asarray(turns))
 
 
 def per_device(reference_signal, surveillance, loading):
     shards = lax.axis_size(TM)
     length = reference_signal.shape[1]
     width = surveillance.shape[1]
-    total = length * shards
-    segments = length // SEG_LEN
-    here = lax.axis_index(TM)
-    pairs = [(i, i + 1) for i in range(shards - 1)]
-    prior = lax.ppermute(reference_signal[:, length - LAGS :], TM, pairs)
-    local, table = first_pass(prior, reference_signal, surveillance, here[None], shards - 1)
-    sums = lax.psum(local, TM)
+    sums, table = first_pass(reference_signal, surveillance)
     weights = solve(sums, loading)
-    corr, energy = second_pass(weights, table, surveillance)
-    power = lax.psum(energy[:width, 0] + energy[width:, 0], TM)
-    scale = lax.rsqrt(total * (power / total + EPSILON))
-    scale = lax.all_gather(scale, "chan", tiled=True)
-    cells = lax.all_to_all(corr[:, None, :], TM_CHAN, split_axis=0, concat_axis=0, tiled=True)
-    cells = cells.reshape(shards, LAGS // shards, corr.shape[1])
-    full = doppler(cells, jnp.broadcast_to(scale[:, None], (scale.shape[0], 128)), segments)
+    cells, energies = second_pass(weights, table, surveillance)
+    full = doppler(cells, energies, length // SEG_LEN, float(length * shards))
     return full, jnp.swapaxes(weights.reshape(2, width, LAGS), 1, 2)
 
 

time: 439 us -> 77.3 us (0.18); the launches traced: 434 us -> 77.1 us
  blocking collectives: 380 us -> 0 us
  Pallas kernels: 32.1 us -> 75.8 us
  starting transfers between devices: 15.6 us -> 0 us
    psum x2 -> x0, blocking collectives: 372 us -> none  [the longest x1 246 us: per_device(): sums = lax.psum(local, TM)]
    pallas_call x3, Pallas kernels: 11.1 us -> 54.8 us  [the longest x1 29.1 us: first_pass(): pl.pallas_call(first_kernel, out_shape=[jax.ShapeDtypeStruct((2,) + part,...]
    all_to_all x1 -> x0, starting transfers between devices: 10.7 us -> none  [per_device(): lax.all_to_all(corr[:, None, :], TM_CHAN, split_axis=0, concat_axis=0, ti...]
    unnamed x1 -> x0, blocking collectives: 8.41 us -> none
    ppermute x1 -> x0, starting transfers between devices: 4.92 us -> none  [per_device(): prior = lax.ppermute(reference_signal[:, length - LAGS:], TM, pairs)]
  transfers between devices with their start and end apart: 2 -> 0, of which waited for: 0 -> 0; matrix products, arithmetic and copies ran while one was open for 1% -> 0% of each run, Pallas kernels for 0% -> 0%
where the time goes in v1:
time: 77.3 us; the launch traced here: 77.1 us
  Pallas kernels  75.8 us (98%)
  between operations  1.29 us (2%)
    pallas_call x1, Pallas kernels, first_pass(): pl.pallas_call(first_kernel, out_shape=[jax.ShapeDtypeStruct((2,) + part,...  29.1 us
    pallas_call x1, Pallas kernels, second_pass(): pl.pallas_call(second_kernel, out_shape=[jax.ShapeDtypeStruct((8, 32, 128...  23.2 us
    pallas_call x1, Pallas kernels, solve(): pl.pallas_call(solve_kernel, out_shape=jax.ShapeDtypeStruct((ROWS - 8, LA...  21 us
    pallas_call x1, Pallas kernels, doppler(): pl.pallas_call(functools.partial(doppler_kernel, samples), out_shape=jax....  2.56 us

profile of v1, /device:TPU:1, one launch (start us, length us, event | category | flops | bytes accessed | tf_op | source)
XLA Modules:
  0.0 77.1 jit_solution(1942088361785256653)
XLA Ops:
  1.3 29.1 %first_pass.1 = (f32[2,40,128]{2,1,0:T(8,128)}, bf16[2,2,128,2304]{3,2,1,0:T(8,128)(2,1)}) custom-call(f32[2,2048]{1,0:T(2,128)} %reference.1, f32[2,16,2048]{2,1,0:T(8,128)} %surveillance.3), custom_call_target="tpu_custom_call" | custom-call | tf_op jit(solution)/shard_map/first_pass/pallas_call | solution.py:171
  30.4 21.0 %solve.1.weights = f32[32,256]{1,0:T(8,128)} custom-call(f32[1]{0:T(128)S(6)} %copy.7.loading, f32[2,40,128]{2,1,0:T(8,128)} %get-tuple-element.6.sums), custom_call_target="tpu_custom_call" | custom-call | tf_op jit(solution)/shard_map/solve/pallas_call | solution.py:385
  51.3 23.2 %second_pass.1 = (f32[8,32,128]{2,1,0:T(8,128)}, f32[8,8,128]{2,1,0:T(8,128)}) custom-call(f32[32,256]{1,0:T(8,128)} %solve.1.weights, bf16[2,2,128,2304]{3,2,1,0:T(8,128)(2,1)} %get-tuple-element.7.table, f32[2,16,2048]{2,1,0:T(8,128)} %surveillance.3), custom_call_target="tpu_custom_call" | custom-call | tf_op jit(solution)/shard_map/second_pass/pallas_call | solution.py:458
  74.6 2.6 %doppler.1 = f32[1,2,64,1024]{3,2,1,0:T(8,128)} custom-call(f32[8,32,128]{2,1,0:T(8,128)} %get-tuple-element.8.cells, f32[8,8,128]{2,1,0:T(8,128)} %get-tuple-element.9.energies, f32[64,512]{1,0:T(8,128)} %constant.4.clone.table, f32[2,4,1024]{2,1,0:T(4,128)} %constant.5.clone.turns), custom_call_target="tpu_custom_call" | custom-call | tf_op jit(solution)/shard_map/doppler/pallas_call | solution.py:531

commit v2 on v1

--- a/solution.py
+++ b/solution.py
@@ -46,7 +46,7 @@
     return pltpu.roll(wide, 0, 1, stride=1, stride_axis=0)
 
 
-def exchange(axes, src, dst, send, recv):
+def exchange(axes, src, dst, send, recv, start=True):
     sizes = [lax.axis_size(a) for a in axes]
     count = int(np.prod(sizes))
     here = place(axes)
@@ -63,7 +63,8 @@
                 device_id_type=MESH,
             )
         )
-        copies[-1].start()
+        if start:
+            copies[-1].start()
     return copies
 
 
@@ -82,112 +83,23 @@
     return coordinates
 
 
-def greet(groups):
-    barrier = pltpu.get_barrier_semaphore()
-    total = 0
-    for axes, offsets in groups:
-        count = int(np.prod([lax.axis_size(a) for a in axes]))
-        here = place(axes)
-        for d in offsets:
-            pl.semaphore_signal(
-                barrier, inc=1, device_id=device(axes, lax.rem(here + d, count)), device_id_type=MESH
-            )
-            total += 1
-    return barrier, total
+def greet(barrier, axes, offsets):
+    count = int(np.prod([lax.axis_size(a) for a in axes]))
+    here = place(axes)
+
+    def one(d):
+        pl.semaphore_signal(
+            barrier, inc=1, device_id=device(axes, lax.rem(here + d, count)), device_id_type=MESH
+        )
+
+    for d in offsets:
+        one(d)
+    return len(offsets)
 
 
 def finish(copies):
     for copy in copies:
         copy.wait()
-
-
-def first_kernel(
-    reference, surveillance, sums, table,
-    halo, mine, pair, ring_y, ring_z, edge_sem, core_send, core_recv, y_send, y_recv, z_send, z_recv, out_send, out_recv,
-):
-    length = reference.shape[1]
-    count = lax.axis_size(TM)
-    here = place(TM)
-    core, y, z = lax.axis_index(TM[2]), lax.axis_index(TM[0]), lax.axis_index(TM[1])
-    barrier, total = greet(
-        [(TM, (1, count - 1)), (TM[2:], (1,)), (TM[:1], (1, 2, 3)), (TM[1:2], tuple(range(1, 8)))]
-    )
-    pl.semaphore_wait(barrier, total)
-    forward = pltpu.make_async_remote_copy(
-        src_ref=reference.at[:, pl.ds(length - LAGS, LAGS)],
-        dst_ref=halo,
-        send_sem=edge_sem.at[0],
-        recv_sem=edge_sem.at[1],
-        device_id=device(TM, lax.rem(here + 1, count)),
-        device_id_type=MESH,
-    )
-    forward.start()
-
-    def fill(tile, part, window):
-        high, low = halves(toeplitz(window, 128)[:, 128:])
-        cut = slice(128 * tile, 128 * tile + 128)
-        table[part, 0, :, cut] = high
-        table[part, 1, :, cut] = low
-
-    for part in range(2):
-        for tile in range(3, (LAGS + length) // 128):
-            fill(tile, part, reference[part : part + 1, 128 * tile - 384 : 128 * tile - 128])
-    s_re, s_im = surveillance[0], surveillance[1]
-    r_re, r_im = reference[0:1], reference[1:2]
-    blank = jnp.zeros((6, length), jnp.float32)
-    with_re = halves(jnp.concatenate([s_re, s_im, r_re, r_im, blank], axis=0))
-    with_im = halves(jnp.concatenate([s_im, -s_re, r_im, -r_re, blank], axis=0))
-    forward.wait()
-    before = jnp.where(here > 0, halo[...], 0.0)
-    for part in range(2):
-        fill(1, part, before[part : part + 1])
-        fill(2, part, jnp.concatenate([before[part : part + 1, 128:], reference[part : part + 1, :128]], axis=1))
-    owner = jnp.where(here == count - 1, 1.0, 0.0)
-    for half in range(2):
-        cut = slice(256 - 128 * half, 256 - 128 * half + length)
-        taps = [[table[part, piece, :, cut] for piece in range(2)] for part in range(2)]
-        product = dot3(taps[0], with_re, NT) + dot3(taps[1], with_im, NT)
-        wide = jnp.concatenate([product, jnp.zeros((128, 128 - ROWS), jnp.float32)], axis=1)
-        mine[half] = wide.T[:ROWS]
-        at = length - LAGS + 128 * half
-        mine[half, 34:36, :] = reference[:, at : at + 128] * owner
-
-    finish(exchange(TM[2:], lambda p: mine.at[p], lambda p: pair, core_send, core_recv))
-    ring_y[y] = mine[core] + pair[...]
-    finish(exchange(TM[:1], lambda p: ring_y.at[y], lambda p: ring_y.at[p], y_send, y_recv))
-    ring_z[z] = (ring_y[0] + ring_y[1]) + (ring_y[2] + ring_y[3])
-    finish(exchange(TM[1:2], lambda p: ring_z.at[z], lambda p: ring_z.at[p], z_send, z_recv))
-    sums[core] = ((ring_z[0] + ring_z[1]) + (ring_z[2] + ring_z[3])) + (
-        (ring_z[4] + ring_z[5]) + (ring_z[6] + ring_z[7])
-    )
-    finish(exchange(TM[2:], lambda p: sums.at[core], lambda p: sums.at[p], out_send, out_recv))
-
-
-def first_pass(reference, surveillance):
-    vmem = pl.BlockSpec(memory_space=pltpu.VMEM)
-    length = reference.shape[1]
-    part = (ROWS, 128)
-    dma = pltpu.SemaphoreType.DMA
-    return pl.pallas_call(
-        first_kernel,
-        out_shape=[
-            jax.ShapeDtypeStruct((2,) + part, jnp.float32),
-            jax.ShapeDtypeStruct((2, 2, 128, LAGS + length), jnp.bfloat16),
-        ],
-        in_specs=[vmem, vmem],
-        out_specs=[vmem, vmem],
-        scratch_shapes=[
-            pltpu.VMEM((2, LAGS), jnp.float32),
-            pltpu.VMEM((2,) + part, jnp.float32),
-            pltpu.VMEM(part, jnp.float32),
-            pltpu.VMEM((4,) + part, jnp.float32),
-            pltpu.VMEM((8,) + part, jnp.float32),
-            dma((2,)),
-            dma((1,)), dma((1,)), dma((3,)), dma((3,)), dma((7,)), dma((7,)), dma((1,)), dma((1,)),
-        ],
-        compiler_params=pltpu.CompilerParams(collective_id=0, has_side_effects=True),
-        name="first_pass",
-    )(reference, surveillance)
 
 
 def times(a, b):
@@ -312,10 +224,11 @@
     return real, imag
 
 
-def invert(real, imag):
+def invert(real, imag, between):
     b = PANEL
 
     def panel(index, carry):
+        between(index)
         start = pl.multiple_of(index * b, b)
         held = pl.ds(start, b)
         top_r, top_i = eliminate(real[held, :], imag[held, :])
@@ -346,7 +259,7 @@
     lax.fori_loop(0, LAGS // b, panel, 0)
 
 
-def normal_matrix(column, loading):
+def normal_matrix(column, tail, loading):
     i0 = lax.broadcasted_iota(jnp.int32, (LAGS, LAGS), 0)
     i1 = lax.broadcasted_iota(jnp.int32, (LAGS, LAGS), 1)
     flip = jnp.where(i0 + i1 == LAGS - 1, 1.0, 0.0)
@@ -356,8 +269,8 @@
     base_r = toeplitz(jnp.concatenate([column[0:1], behind[0:1]], axis=1), LAGS)[:, :LAGS]
     base_i = toeplitz(jnp.concatenate([-column[1:2], behind[1:2]], axis=1), LAGS)[:, :LAGS]
     blank = jnp.zeros((1, LAGS), jnp.float32)
-    edge_r = toeplitz(jnp.concatenate([blank, column[2:3]], axis=1), LAGS)[:, :LAGS]
-    edge_i = toeplitz(jnp.concatenate([blank, column[3:4]], axis=1), LAGS)[:, :LAGS]
+    edge_r = toeplitz(jnp.concatenate([blank, tail[0:1]], axis=1), LAGS)[:, :LAGS]
+    edge_i = toeplitz(jnp.concatenate([blank, tail[1:2]], axis=1), LAGS)[:, :LAGS]
     one = jnp.concatenate([edge_r, edge_i], axis=1)
     two = jnp.concatenate([edge_i, -edge_r], axis=1)
     real = base_r - dot(one, one, NT)
@@ -367,43 +280,147 @@
     return jnp.where(diagonal, real + lam, real), imag
 
 
-def solve_kernel(loading, sums, weights, real, imag):
-    joined = jnp.concatenate([sums[0], sums[1]], axis=1)
-    start_r, start_i = normal_matrix(joined[32:40, :], loading[0])
+PAIR, FAR, NEAR = TM[2:], TM[:2], (TM[2], "chan")
+ALONG_Y, ALONG_Z = TM[:1], TM[1:2]
+
+
+def cancel_kernel(
+    loading, reference, surveillance, weights, cells, energies,
+    table, halo, tail, mine, gram_pair, gram_all, real, imag,
+    pair, ring_y, ring_z, cross, corr, landed, turned, power, power_z, power_y,
+    edge_sem, tail_send, tail_recv, gram_sem, gram_send, gram_recv,
+    pair_sem, y_send, y_recv, z_send, z_recv, out_sem,
+    far_send, far_recv, near_send, near_recv, pz_send, pz_recv, py_send, py_recv, pa_send, pa_recv,
+):
+    length = reference.shape[1]
+    width = surveillance.shape[1]
+    count = lax.axis_size(TM)
+    here = place(TM)
+    core, y, z, far, near = place(PAIR), place(ALONG_Y), place(ALONG_Z), place(FAR), place(NEAR)
+    barrier = pltpu.get_barrier_semaphore()
+    total = greet(barrier, TM, range(1, count))
+    total += greet(barrier, NEAR, [d for d in range(1, 8) if d != 4])
+
+    def fill(tile, part, window):
+        high, low = halves(toeplitz(window, 128)[:, 128:])
+        cut = slice(128 * tile, 128 * tile + 128)
+        table[part, 0, :, cut] = high
+        table[part, 1, :, cut] = low
+
+    for part in range(2):
+        for tile in range(3, (LAGS + length) // 128):
+            fill(tile, part, reference[part : part + 1, 128 * tile - 384 : 128 * tile - 128])
+
+    pl.semaphore_wait(barrier, total)
+    forward = pltpu.make_async_remote_copy(
+        src_ref=reference.at[:, pl.ds(length - LAGS, LAGS)],
+        dst_ref=halo,
+        send_sem=edge_sem.at[0],
+        recv_sem=edge_sem.at[1],
+        device_id=device(TM, lax.rem(here + 1, count)),
+        device_id_type=MESH,
+    )
+    forward.start()
+    source = reference.at[:, pl.ds(length - LAGS, LAGS)]
+
+    def tail_copy(d, semaphore):
+        return pltpu.make_async_remote_copy(
+            src_ref=source,
+            dst_ref=tail,
+            send_sem=tail_send.at[semaphore],
+            recv_sem=tail_recv.at[0],
+            device_id=device(TM, lax.rem(here + d, count)),
+            device_id_type=MESH,
+        )
+
+    @pl.when(here == count - 1)
+    def _():
+        tail[...] = reference[:, length - LAGS :]
+        for d in range(1, count):
+            tail_copy(d, d - 1).start()
+
+    s_re, s_im = surveillance[0], surveillance[1]
+    r_re, r_im = reference[0:1], reference[1:2]
+    blank = jnp.zeros((6, length), jnp.float32)
+    with_re = halves(jnp.concatenate([s_re, s_im, r_re, r_im, blank], axis=0))
+    with_im = halves(jnp.concatenate([s_im, -s_re, r_im, -r_re, blank], axis=0))
+    forward.wait()
+    before = jnp.where(here > 0, halo[...], 0.0)
+    for part in range(2):
+        fill(1, part, before[part : part + 1])
+        fill(2, part, jnp.concatenate([before[part : part + 1, 128:], reference[part : part + 1, :128]], axis=1))
+
+    for half in range(2):
+        cut = slice(256 - 128 * half, 256 - 128 * half + length)
+        taps = [[table[part, piece, :, cut] for piece in range(2)] for part in range(2)]
+        sums = dot3(taps[0], with_re, NT) + dot3(taps[1], with_im, NT)
+        sums = jnp.concatenate([sums, jnp.zeros((128, 128 - ROWS), jnp.float32)], axis=1).T
+        mine[half] = sums[: 2 * width]
+        gram_pair[0, half : half + 1, :] = sums[2 * width : 2 * width + 1]
+        gram_pair[0, 2 + half : 3 + half, :] = sums[2 * width + 1 : 2 * width + 2]
+    finish(exchange(PAIR, lambda p: gram_pair.at[0], lambda p: gram_pair.at[1], gram_sem.at[0:1], gram_sem.at[1:2]))
+    gram_all[far] = gram_pair[0] + gram_pair[1]
+    to_gram = exchange(FAR, lambda p: gram_all.at[far], lambda p: gram_all.at[p], gram_send, gram_recv)
+    exchange(PAIR, lambda p: mine.at[p], lambda p: pair, pair_sem.at[0:1], pair_sem.at[1:2])
+
+    @pl.when(here == count - 1)
+    def _():
+        for d in range(1, count):
+            tail_copy(d, d - 1).wait_send()
+
+    @pl.when(here != count - 1)
+    def _():
+        tail_copy(1, 0).wait_recv()
+
+    finish(to_gram)
+    gram = jnp.sum(gram_all[...], axis=0)
+    column = jnp.concatenate([gram[0:1], gram[1:2]], axis=1)
+    column = jnp.concatenate([column, jnp.concatenate([gram[2:3], gram[3:4]], axis=1)], axis=0)
+    column = jnp.concatenate([column, jnp.zeros((6, LAGS), jnp.float32)], axis=0)
+    start_r, start_i = normal_matrix(column, tail[...], loading[0])
     real[...] = start_r
     imag[...] = start_i
-    invert(real, imag)
-    half = (ROWS - 8) // 2
-    c_re, c_im = joined[:half, :], joined[half : 2 * half, :]
-    weights[...] = dot(joined[: 2 * half, :], real[...], NT) + dot(
-        jnp.concatenate([-c_im, c_re], axis=0), imag[...], NT
-    )
-
-
-def solve(sums, loading):
-    vmem = pl.BlockSpec(memory_space=pltpu.VMEM)
-    return pl.pallas_call(
-        solve_kernel,
-        out_shape=jax.ShapeDtypeStruct((ROWS - 8, LAGS), jnp.float32),
-        in_specs=[pl.BlockSpec(memory_space=pltpu.SMEM), vmem],
-        out_specs=vmem,
-        scratch_shapes=[pltpu.VMEM((LAGS, LAGS), jnp.float32)] * 2,
-        name="solve",
-    )(loading, sums)
-
-
-def second_kernel(
-    weights, table, surveillance, cells, energies,
-    corr, landed, turned, power, ring_z, ring_y,
-    far_send, far_recv, near_send, near_recv, z_send, z_recv, y_send, y_recv, e_send, e_recv,
-):
-    length = surveillance.shape[2]
-    width = surveillance.shape[1]
-    far, near = TM[:2], (TM[2], "chan")
-    z, y, me_far, me_near = place(TM[1:2]), place(TM[:1]), place(far), place(near)
-    barrier, total = greet([(far, tuple(range(1, 32))), (near, tuple(range(1, 8))), (TM[1:2], tuple(range(1, 8))), (TM[:1], (1, 2, 3))])
-    pl.semaphore_wait(barrier, total)
-    w = weights[...]
+
+    def pair_copy(start):
+        return exchange(PAIR, lambda p: mine.at[p], lambda p: pair, pair_sem.at[0:1], pair_sem.at[1:2], start)
+
+    def y_copy(start):
+        return exchange(ALONG_Y, lambda p: ring_y.at[y], lambda p: ring_y.at[p], y_send, y_recv, start)
+
+    def z_copy(start):
+        return exchange(ALONG_Z, lambda p: ring_z.at[z], lambda p: ring_z.at[p], z_send, z_recv, start)
+
+    def out_copy(start):
+        return exchange(PAIR, lambda p: cross.at[core], lambda p: cross.at[p], out_sem.at[0:1], out_sem.at[1:2], start)
+
+    def between(index):
+        @pl.when(index == 1)
+        def _():
+            finish(pair_copy(False))
+            ring_y[y] = mine[core] + pair[...]
+            y_copy(True)
+
+        @pl.when(index == 3)
+        def _():
+            finish(y_copy(False))
+            ring_z[z] = (ring_y[0] + ring_y[1]) + (ring_y[2] + ring_y[3])
+            z_copy(True)
+
+        @pl.when(index == 6)
+        def _():
+            finish(z_copy(False))
+            cross[core] = ((ring_z[0] + ring_z[1]) + (ring_z[2] + ring_z[3])) + (
+                (ring_z[4] + ring_z[5]) + (ring_z[6] + ring_z[7])
+            )
+            out_copy(True)
+
+    invert(real, imag, between)
+    finish(out_copy(False))
+    right = jnp.concatenate([cross[0], cross[1]], axis=1)
+    spun = jnp.concatenate([-right[width:], right[:width]], axis=0)
+    w = dot(right, real[...], NT) + dot(spun, imag[...], NT)
+    weights[...] = w
+
     w_re, w_im = w[:width], w[width:]
     on_re = halves(w)
     on_im = halves(jnp.concatenate([-w_im, w_re], axis=0))
@@ -419,8 +436,8 @@
     energy = jnp.sum(residual * residual, axis=1, keepdims=True)
     energy = jnp.broadcast_to(energy[:width] + energy[width:], (width, 128))
     energy = jnp.concatenate([energy, jnp.zeros((128 - width, 128), jnp.float32)], axis=0)
-    ring_z[z] = energy.T[:8]
-    along_z = exchange(TM[1:2], lambda p: ring_z.at[z], lambda p: ring_z.at[p], z_send, z_recv)
+    power_z[z] = energy.T[:8]
+    along_z = exchange(ALONG_Z, lambda p: power_z.at[z], lambda p: power_z.at[p], pz_send, pz_recv)
     swapped = jnp.concatenate([residual[width:], -residual[:width]], axis=0)
     segments = length // SEG_LEN
     row = lax.broadcasted_iota(jnp.int32, (2 * width * segments, length), 0)
@@ -431,50 +448,58 @@
     for half in range(2):
         block = dot3(taps[half][0], with_re, NT) + dot3(taps[half][1], with_im, NT)
         corr[16 * half : 16 * half + 16] = block.reshape(16, 8, 128)
-    to_far = exchange(far, lambda p: corr.at[p], lambda p: landed.at[p], far_send, far_recv)
-    landed[me_far] = corr[me_far]
+
+    to_far = exchange(FAR, lambda p: corr.at[p], lambda p: landed.at[p], far_send, far_recv)
+    landed[far] = corr[far]
     finish(along_z)
-    parts = [ring_z[i] for i in range(8)]
-    ring_y[y] = ((parts[0] + parts[1]) + (parts[2] + parts[3])) + ((parts[4] + parts[5]) + (parts[6] + parts[7]))
-    along_y = exchange(TM[:1], lambda p: ring_y.at[y], lambda p: ring_y.at[p], y_send, y_recv)
-    finish(along_y)
-    power[...] = (ring_y[0] + ring_y[1]) + (ring_y[2] + ring_y[3])
-    energies[me_near] = power[...]
-    to_all = exchange(near, lambda p: power, lambda p: energies.at[p], e_send, e_recv)
+    parts = [power_z[i] for i in range(8)]
+    power_y[y] = ((parts[0] + parts[1]) + (parts[2] + parts[3])) + ((parts[4] + parts[5]) + (parts[6] + parts[7]))
+    finish(exchange(ALONG_Y, lambda p: power_y.at[y], lambda p: power_y.at[p], py_send, py_recv))
+    power[...] = (power_y[0] + power_y[1]) + (power_y[2] + power_y[3])
+    energies[near] = power[...]
+    to_all = exchange(NEAR, lambda p: power, lambda p: energies.at[p], pa_send, pa_recv)
     finish(to_far)
     everything = landed[...]
     for lag in range(8):
         turned[lag] = everything[:, lag, :]
-    to_near = exchange(near, lambda p: turned.at[p], lambda p: cells.at[p], near_send, near_recv)
-    cells[me_near] = turned[me_near]
+    to_near = exchange(NEAR, lambda p: turned.at[p], lambda p: cells.at[p], near_send, near_recv)
+    cells[near] = turned[near]
     finish(to_all)
     finish(to_near)
 
 
-def second_pass(weights, table, surveillance):
+def cancel(loading, reference, surveillance):
     vmem = pl.BlockSpec(memory_space=pltpu.VMEM)
+    length = reference.shape[1]
+    width = surveillance.shape[1]
     dma = pltpu.SemaphoreType.DMA
-    f32 = jnp.float32
+
+    def block(*shape):
+        return pltpu.VMEM(shape, jnp.float32)
+
+    half = (2 * width, 128)
     return pl.pallas_call(
-        second_kernel,
+        cancel_kernel,
         out_shape=[
-            jax.ShapeDtypeStruct((8, 32, 128), f32),
-            jax.ShapeDtypeStruct((8, 8, 128), f32),
+            jax.ShapeDtypeStruct((2 * width, LAGS), jnp.float32),
+            jax.ShapeDtypeStruct((8, 32, 128), jnp.float32),
+            jax.ShapeDtypeStruct((8, 8, 128), jnp.float32),
         ],
-        in_specs=[vmem] * 3,
-        out_specs=[vmem] * 2,
+        in_specs=[pl.BlockSpec(memory_space=pltpu.SMEM), vmem, vmem],
+        out_specs=[vmem] * 3,
         scratch_shapes=[
-            pltpu.VMEM((32, 8, 128), f32),
-            pltpu.VMEM((32, 8, 128), f32),
-            pltpu.VMEM((8, 32, 128), f32),
-            pltpu.VMEM((8, 128), f32),
-            pltpu.VMEM((8, 8, 128), f32),
-            pltpu.VMEM((4, 8, 128), f32),
+            pltpu.VMEM((2, 2, 128, LAGS + length), jnp.bfloat16),
+            block(2, LAGS), block(2, LAGS), block(2, *half), block(2, 4, 128), block(32, 4, 128),
+            block(LAGS, LAGS), block(LAGS, LAGS),
+            block(*half), block(4, *half), block(8, *half), block(2, *half),
+            block(32, 8, 128), block(32, 8, 128), block(8, 32, 128), block(8, 128), block(8, 8, 128), block(4, 8, 128),
+            dma((2,)), dma((63,)), dma((1,)), dma((2,)), dma((31,)), dma((31,)),
+            dma((2,)), dma((3,)), dma((3,)), dma((7,)), dma((7,)), dma((2,)),
             dma((31,)), dma((31,)), dma((7,)), dma((7,)), dma((7,)), dma((7,)), dma((3,)), dma((3,)), dma((7,)), dma((7,)),
         ],
-        compiler_params=pltpu.CompilerParams(collective_id=1, has_side_effects=True),
-        name="second_pass",
-    )(weights, table, surveillance)
+        compiler_params=pltpu.CompilerParams(collective_id=0, has_side_effects=True),
+        name="cancel",
+    )(loading, reference, surveillance)
 
 
 def doppler_tables(shards, segments):
@@ -538,13 +563,11 @@
 
 
 def per_device(reference_signal, surveillance, loading):
-    shards = lax.axis_size(TM)
     length = reference_signal.shape[1]
     width = surveillance.shape[1]
-    sums, table = first_pass(reference_signal, surveillance)
-    weights = solve(sums, loading)
-    cells, energies = second_pass(weights, table, surveillance)
-    full = doppler(cells, energies, length // SEG_LEN, float(length * shards))
+    samples = float(length * lax.axis_size(TM))
+    weights, cells, energies = cancel(loading, reference_signal, surveillance)
+    full = doppler(cells, energies, length // SEG_LEN, samples)
     return full, jnp.swapaxes(weights.reshape(2, width, LAGS), 1, 2)
 
 

time: 77.3 us -> 68.2 us (0.88)
  Pallas kernels: 75.8 us -> 66.2 us
    pallas_call x3 -> x1, Pallas kernels: 73.3 us -> 63.6 us  [cancel(): pl.pallas_call(cancel_kernel, out_shape=[jax.ShapeDtypeStruct((2 * width,...]
where the time goes in v2:
time: 68.2 us; the launch traced here: 68.1 us
  Pallas kernels  66.2 us (97%)
  between operations  1.29 us (2%)
    pallas_call x1, Pallas kernels, cancel(): pl.pallas_call(cancel_kernel, out_shape=[jax.ShapeDtypeStruct((2 * width,...  63.6 us
    pallas_call x1, Pallas kernels, doppler(): pl.pallas_call(functools.partial(doppler_kernel, samples), out_shape=jax....  2.56 us

profile of v2, /device:TPU:1, one launch (start us, length us, event | category | flops | bytes accessed | tf_op | source)
XLA Modules:
  0.0 68.1 jit_solution(1157558582500698701)
XLA Ops:
  1.3 63.6 %cancel.1 = (f32[32,256]{1,0:T(8,128)}, f32[8,32,128]{2,1,0:T(8,128)}, f32[8,8,128]{2,1,0:T(8,128)}) custom-call(f32[1]{0:T(128)S(6)} %copy.8.loading, f32[2,2048]{1,0:T(2,128)} %reference.1, f32[2,16,2048]{2,1,0:T(8,128)} %surveillance.1), custom_call_target="tpu_custom_call" | custom-call | tf_op jit(solution)/shard_map/cancel/pallas_call | solution.py:481
  64.9 0.0 copy-start
  64.9 2.6 %doppler.1 = f32[1,2,64,1024]{3,2,1,0:T(8,128)} custom-call(f32[8,32,128]{2,1,0:T(8,128)} %get-tuple-element.5.cells, f32[8,8,128]{2,1,0:T(8,128)} %get-tuple-element.6.energies, f32[64,512]{1,0:T(8,128)} %constant.4.clone.table, f32[2,4,1024]{2,1,0:T(4,128)} %constant.5.clone.turns), custom_call_target="tpu_custom_call" | custom-call | tf_op jit(solution)/shard_map/doppler/pallas_call | solution.py:556
  67.5 0.0 copy-done
  67.5 0.6 copy.9
Async XLA Ops:
  64.9 2.6 %copy-start = (f32[32,256]{1,0:T(8,128)S(1)}, f32[32,256]{1,0:T(8,128)}, u32[]{:S(2)}) copy-start(f32[32,256]{1,0:T(8,128)} %get-tuple-element.7) | copy-start | bytes 98308

commit v3 on v2

--- a/solution.py
+++ b/solution.py
@@ -39,6 +39,19 @@
         return lax.dot_general(x, y, dims, preferred_element_type=jnp.float32)
 
     return one(a[0], b[0]) + (one(a[0], b[1]) + one(a[1], b[0]))
+
+
+def dot_beside(a, b):
+    both = lax.dot_general(a[0], jnp.concatenate(b, axis=0), NT, preferred_element_type=jnp.float32)
+    rest = lax.dot_general(a[1], b[0], NT, preferred_element_type=jnp.float32)
+    return both[:, :128] + (both[:, 128:] + rest)
+
+
+def dot_stacked(a, b):
+    rows = a[0].shape[0]
+    both = lax.dot_general(jnp.concatenate(a, axis=0), b[0], NN, preferred_element_type=jnp.float32)
+    rest = lax.dot_general(a[0], b[1], NN, preferred_element_type=jnp.float32)
+    return both[:rows] + (both[rows:] + rest)
 
 
 def toeplitz(row, rows):
@@ -175,7 +188,13 @@
     return [first[i] + right[i] for i in range(half)] + [below[i] + rest_inverse[i] for i in range(half)]
 
 
-def eliminate(real, imag):
+def added(terms):
+    while len(terms) > 1:
+        terms = [sum(terms[i : i + 2][1:], terms[i]) for i in range(0, len(terms), 2)]
+    return terms[0]
+
+
+def eliminate(real, imag, first):
     height, n = real.shape
     m = PIVOTS
     lane = lax.broadcasted_iota(jnp.int32, (1, n), 1)
@@ -186,17 +205,18 @@
         return None if value is None else jnp.concatenate([value] * (n // 128), axis=1)
 
     for k in range(0, height, m):
-        col_r = [jnp.broadcast_to(real[:, k + j : k + j + 1], (height, 128)) for j in range(m)]
-        col_i = [jnp.broadcast_to(imag[:, k + j : k + j + 1], (height, 128)) for j in range(m)]
+        at = first + k
+        col_r = [jnp.broadcast_to(real[:, at + j : at + j + 1], (height, 128)) for j in range(m)]
+        col_i = [jnp.broadcast_to(imag[:, at + j : at + j + 1], (height, 128)) for j in range(m)]
         block = [
             [(col_r[j][k + i : k + i + 1], col_i[j][k + i : k + i + 1]) for j in range(m)]
             for i in range(m)
         ]
         inverse = [[(wide(q[0]), wide(q[1])) for q in row] for row in hermitian_inverse(block)]
-        hit = (lane >= k) & (lane < k + m)
+        hit = (lane >= at) & (lane < at + m)
         old = [
             (
-                jnp.where(hit, jnp.where(lane == k + i, 1.0, 0.0), real[k + i : k + i + 1]),
+                jnp.where(hit, jnp.where(lane == at + i, 1.0, 0.0), real[k + i : k + i + 1]),
                 jnp.where(hit, 0.0, imag[k + i : k + i + 1]),
             )
             for i in range(m)
@@ -206,60 +226,114 @@
         inside = (rows >= k) & (rows < k + m)
         col_r = [jnp.where(inside, jnp.where(rows == k + j, -1.0, 0.0), col_r[j]) for j in range(m)]
         col_i = [jnp.where(inside, 0.0, col_i[j]) for j in range(m)]
-        gone = inside | ((lanes >= k) & (lanes < k + m))
+        gone = inside | ((lanes >= at % 128) & (lanes < at % 128 + m))
         out_r, out_i = [], []
         for t in range(n // 128):
             cut = slice(128 * t, 128 * t + 128)
-            mask = gone if t == 0 else inside
+            mask = gone if t == at // 128 else inside
             next_r = jnp.where(mask, 0.0, real[:, cut])
             next_i = jnp.where(mask, 0.0, imag[:, cut])
+            terms_r, terms_i = [], []
             for j in range(m):
                 row_r, row_i = new[j][0][:, cut], new[j][1][:, cut]
-                next_r = next_r - (col_r[j] * row_r - col_i[j] * row_i)
-                next_i = next_i - (col_r[j] * row_i + col_i[j] * row_r)
-            out_r.append(next_r)
-            out_i.append(next_i)
+                terms_r.append(col_r[j] * row_r - col_i[j] * row_i)
+                terms_i.append(col_r[j] * row_i + col_i[j] * row_r)
+            out_r.append(next_r - added(terms_r))
+            out_i.append(next_i - added(terms_i))
         real = jnp.concatenate(out_r, axis=1)
         imag = jnp.concatenate(out_i, axis=1)
     return real, imag
 
 
+def thirds(x):
+    high = x.astype(jnp.bfloat16)
+    rest = x - high.astype(jnp.float32)
+    middle = rest.astype(jnp.bfloat16)
+    return high, middle, (rest - middle.astype(jnp.float32)).astype(jnp.bfloat16)
+
+
+def packed(factor, top_r, top_i, first):
+    turned = first // PANEL
+    high, middle, low = [
+        [x[:PANEL], x[PANEL:]]
+        for x in thirds(
+            jnp.concatenate(
+                [jnp.concatenate([top_r, top_i], axis=1), jnp.concatenate([-top_i, top_r], axis=1)], axis=0
+            )
+        )
+    ]
+    blocks = []
+    for pieces in (high + middle, low + high, middle + high):
+        blocks += pieces[4 - turned :] + pieces[: 4 - turned]
+    right = jnp.concatenate(blocks, axis=0)
+    high = factor.astype(jnp.bfloat16).astype(jnp.float32)
+    rest = factor - high
+    middle = rest.astype(jnp.bfloat16).astype(jnp.float32)
+    low = rest - middle
+    left = [high + pltpu.roll(high, 64, 1), high + pltpu.roll(middle, 64, 1), middle + pltpu.roll(low, 64, 1)]
+    left = jnp.concatenate(left, axis=1).astype(jnp.bfloat16)
+    return lax.dot_general(left, right, NN, preferred_element_type=jnp.float32)
+
+
+def factors(real, imag, first):
+    lane = lax.broadcasted_iota(jnp.int32, real.shape, 1)
+    behind = (first + PANEL) % 128
+    in_r = (lane >= first) & (lane < first + PANEL)
+    in_i = (lane >= behind) & (lane < behind + PANEL)
+    return jnp.where(in_r, real, jnp.where(in_i, pltpu.roll(imag, PANEL, 1), 0.0))
+
+
+def without(x, first):
+    tile = first // 128
+    cut = x[:, 128 * tile : 128 * tile + 128]
+    lane = lax.broadcasted_iota(jnp.int32, cut.shape, 1) + 128 * tile
+    cut = jnp.where((lane >= first) & (lane < first + PANEL), 0.0, cut)
+    return jnp.concatenate([cut, x[:, 128:]] if tile == 0 else [x[:, :128], cut], axis=1)
+
+
 def invert(real, imag, between):
     b = PANEL
-
-    def panel(index, carry):
-        between(index)
-        start = pl.multiple_of(index * b, b)
-        held = pl.ds(start, b)
-        top_r, top_i = eliminate(real[held, :], imag[held, :])
-        all_r, all_i = real[...], imag[...]
-        lane = lax.broadcasted_iota(jnp.int32, (LAGS, 128), 1)
-        row = lax.broadcasted_iota(jnp.int32, (LAGS, 128), 0)
-        factor = jnp.where(lane < b, all_r[:, :128], pltpu.roll(all_i[:, :128], b, 1))
-        inside = (row >= start) & (row < start + b)
-        factor = jnp.where(inside | (lane >= 2 * b), 0.0, factor)
-        right = jnp.concatenate(
-            [
-                jnp.concatenate([top_r, top_i], axis=1),
-                jnp.concatenate([-top_i, top_r], axis=1),
-                jnp.zeros((128 - 2 * b, 2 * LAGS), jnp.float32),
-            ],
-            axis=0,
-        )
-        update = dot(factor, right)
-        column = lax.broadcasted_iota(jnp.int32, (LAGS, LAGS), 1)
-        all_r = jnp.where(column < b, 0.0, all_r) - update[:, :LAGS]
-        all_i = jnp.where(column < b, 0.0, all_i) - update[:, LAGS:]
-        real[...] = pltpu.roll(all_r, LAGS - b, 1)
-        imag[...] = pltpu.roll(all_i, LAGS - b, 1)
-        real[held, :] = pltpu.roll(top_r, LAGS - b, 1)
-        imag[held, :] = pltpu.roll(top_i, LAGS - b, 1)
-        return carry
-
-    lax.fori_loop(0, LAGS // b, panel, 0)
-
-
-def normal_matrix(column, tail, loading):
+    panels = LAGS // b
+
+    def update(rows, last, done):
+        first = last * b
+        tile = slice(first // 128 * 128, first // 128 * 128 + 128)
+        old_r, old_i = real[rows, :], imag[rows, :]
+        change = packed(factors(old_r[:, tile], old_i[:, tile], first % 128), *done, first % 128)
+        return without(old_r, first) - change[:, :LAGS], without(old_i, first) - change[:, LAGS:]
+
+    def apply(last, done):
+        held = slice(last * b, last * b + b)
+        new_r, new_i = update(slice(0, LAGS), last, done)
+        for rows in (slice(0, last * b), slice(last * b + b, LAGS)):
+            if rows.start < rows.stop:
+                real[rows, :] = new_r[rows]
+                imag[rows, :] = new_i[rows]
+        real[held, :] = done[0]
+        imag[held, :] = done[1]
+
+    top = (real[:b, :], imag[:b, :])
+    done = None
+    for p in range(panels):
+        between(p)
+        if done is not None:
+            apply(p - 1, done)
+        done = eliminate(*top, p * b)
+        if p + 1 < panels:
+            top = update(slice(p * b + b, p * b + 2 * b), p, done)
+    apply(panels - 1, done)
+
+
+def edge_matrix(tail):
+    blank = jnp.zeros((1, LAGS), jnp.float32)
+    edge_r = toeplitz(jnp.concatenate([blank, tail[0:1]], axis=1), LAGS)[:, :LAGS]
+    edge_i = toeplitz(jnp.concatenate([blank, tail[1:2]], axis=1), LAGS)[:, :LAGS]
+    one = jnp.concatenate([edge_r, edge_i], axis=1)
+    two = jnp.concatenate([edge_i, -edge_r], axis=1)
+    return dot(one, one, NT), dot(one, two, NT)
+
+
+def normal_matrix(column, edge_r, edge_i, loading):
     i0 = lax.broadcasted_iota(jnp.int32, (LAGS, LAGS), 0)
     i1 = lax.broadcasted_iota(jnp.int32, (LAGS, LAGS), 1)
     flip = jnp.where(i0 + i1 == LAGS - 1, 1.0, 0.0)
@@ -268,16 +342,11 @@
     behind = jnp.where(lane == 0, 0.0, behind)
     base_r = toeplitz(jnp.concatenate([column[0:1], behind[0:1]], axis=1), LAGS)[:, :LAGS]
     base_i = toeplitz(jnp.concatenate([-column[1:2], behind[1:2]], axis=1), LAGS)[:, :LAGS]
-    blank = jnp.zeros((1, LAGS), jnp.float32)
-    edge_r = toeplitz(jnp.concatenate([blank, tail[0:1]], axis=1), LAGS)[:, :LAGS]
-    edge_i = toeplitz(jnp.concatenate([blank, tail[1:2]], axis=1), LAGS)[:, :LAGS]
-    one = jnp.concatenate([edge_r, edge_i], axis=1)
-    two = jnp.concatenate([edge_i, -edge_r], axis=1)
-    real = base_r - dot(one, one, NT)
-    imag = base_i - dot(one, two, NT)
     diagonal = i0 == i1
-    lam = loading * (jnp.sum(jnp.where(diagonal, real, 0.0)) / LAGS)
-    return jnp.where(diagonal, real + lam, real), imag
+    off = jnp.sum(jnp.sum(jnp.where(diagonal, edge_r, 0.0), axis=0, keepdims=True), axis=1, keepdims=True)
+    lam = loading * (column[0:1, 0:1] - off / LAGS)
+    real = base_r - edge_r
+    return jnp.where(diagonal, real + lam, real), base_i - edge_i
 
 
 PAIR, FAR, NEAR = TM[2:], TM[:2], (TM[2], "chan")
@@ -301,15 +370,24 @@
     total = greet(barrier, TM, range(1, count))
     total += greet(barrier, NEAR, [d for d in range(1, 8) if d != 4])
 
-    def fill(tile, part, window):
-        high, low = halves(toeplitz(window, 128)[:, 128:])
-        cut = slice(128 * tile, 128 * tile + 128)
-        table[part, 0, :, cut] = high
-        table[part, 1, :, cut] = low
-
-    for part in range(2):
-        for tile in range(3, (LAGS + length) // 128):
-            fill(tile, part, reference[part : part + 1, 128 * tile - 384 : 128 * tile - 128])
+    sums = [[jnp.zeros((128, 128), jnp.float32)] * 2 for _ in range(2)]
+
+    def fill(tile, windows):
+        delayed = [toeplitz(x, 128)[:, 128:] for x in windows]
+        at = slice(128 * tile, 128 * tile + 128)
+        for part in range(2):
+            high, low = halves(delayed[part])
+            table[part, 0, :, at] = high
+            table[part, 1, :, at] = low
+        for half in range(2):
+            start = 128 * (tile - 2 + half)
+            if 0 <= start < length:
+                now_r, now_i = reference[0:1, start : start + 128], reference[1:2, start : start + 128]
+                sums[half][0] = sums[half][0] + (delayed[0] * now_r + delayed[1] * now_i)
+                sums[half][1] = sums[half][1] + (delayed[0] * now_i - delayed[1] * now_r)
+
+    for tile in range(3, (LAGS + length) // 128):
+        fill(tile, [reference[part : part + 1, 128 * tile - 384 : 128 * tile - 128] for part in range(2)])
 
     pl.semaphore_wait(barrier, total)
     forward = pltpu.make_async_remote_copy(
@@ -339,28 +417,26 @@
         for d in range(1, count):
             tail_copy(d, d - 1).start()
 
-    s_re, s_im = surveillance[0], surveillance[1]
-    r_re, r_im = reference[0:1], reference[1:2]
-    blank = jnp.zeros((6, length), jnp.float32)
-    with_re = halves(jnp.concatenate([s_re, s_im, r_re, r_im, blank], axis=0))
-    with_im = halves(jnp.concatenate([s_im, -s_re, r_im, -r_re, blank], axis=0))
     forward.wait()
     before = jnp.where(here > 0, halo[...], 0.0)
-    for part in range(2):
-        fill(1, part, before[part : part + 1])
-        fill(2, part, jnp.concatenate([before[part : part + 1, 128:], reference[part : part + 1, :128]], axis=1))
-
+    fill(1, [before[part : part + 1] for part in range(2)])
+    fill(2, [jnp.concatenate([before[part : part + 1, 128:], reference[part : part + 1, :128]], axis=1) for part in range(2)])
+    for half in range(2):
+        for part in range(2):
+            line = jnp.sum(sums[half][part].T, axis=0, keepdims=True)
+            gram_pair[0, 2 * part + half : 2 * part + half + 1, :] = line
+    finish(exchange(PAIR, lambda p: gram_pair.at[0], lambda p: gram_pair.at[1], gram_sem.at[0:1], gram_sem.at[1:2]))
+    gram_all[far] = gram_pair[0] + gram_pair[1]
+    to_gram = exchange(FAR, lambda p: gram_all.at[far], lambda p: gram_all.at[p], gram_send, gram_recv)
+
+    s_re, s_im = surveillance[0], surveillance[1]
+    blank = jnp.zeros((128 - 2 * width, length), jnp.float32)
+    with_re = halves(jnp.concatenate([s_re, s_im, blank], axis=0))
+    with_im = halves(jnp.concatenate([s_im, -s_re, blank], axis=0))
     for half in range(2):
         cut = slice(256 - 128 * half, 256 - 128 * half + length)
         taps = [[table[part, piece, :, cut] for piece in range(2)] for part in range(2)]
-        sums = dot3(taps[0], with_re, NT) + dot3(taps[1], with_im, NT)
-        sums = jnp.concatenate([sums, jnp.zeros((128, 128 - ROWS), jnp.float32)], axis=1).T
-        mine[half] = sums[: 2 * width]
-        gram_pair[0, half : half + 1, :] = sums[2 * width : 2 * width + 1]
-        gram_pair[0, 2 + half : 3 + half, :] = sums[2 * width + 1 : 2 * width + 2]
-    finish(exchange(PAIR, lambda p: gram_pair.at[0], lambda p: gram_pair.at[1], gram_sem.at[0:1], gram_sem.at[1:2]))
-    gram_all[far] = gram_pair[0] + gram_pair[1]
-    to_gram = exchange(FAR, lambda p: gram_all.at[far], lambda p: gram_all.at[p], gram_send, gram_recv)
+        mine[half] = (dot_beside(taps[0], with_re) + dot_beside(taps[1], with_im)).T[: 2 * width]
     exchange(PAIR, lambda p: mine.at[p], lambda p: pair, pair_sem.at[0:1], pair_sem.at[1:2])
 
     @pl.when(here == count - 1)
@@ -372,12 +448,15 @@
     def _():
         tail_copy(1, 0).wait_recv()
 
+    edge_r, edge_i = edge_matrix(tail[...])
+    real[...] = edge_r
+    imag[...] = edge_i
     finish(to_gram)
     gram = jnp.sum(gram_all[...], axis=0)
     column = jnp.concatenate([gram[0:1], gram[1:2]], axis=1)
     column = jnp.concatenate([column, jnp.concatenate([gram[2:3], gram[3:4]], axis=1)], axis=0)
     column = jnp.concatenate([column, jnp.zeros((6, LAGS), jnp.float32)], axis=0)
-    start_r, start_i = normal_matrix(column, tail[...], loading[0])
+    start_r, start_i = normal_matrix(column, real[...], imag[...], loading[0])
     real[...] = start_r
     imag[...] = start_i
 
@@ -394,20 +473,15 @@
         return exchange(PAIR, lambda p: cross.at[core], lambda p: cross.at[p], out_sem.at[0:1], out_sem.at[1:2], start)
 
     def between(index):
-        @pl.when(index == 1)
-        def _():
+        if index == 1:
             finish(pair_copy(False))
             ring_y[y] = mine[core] + pair[...]
             y_copy(True)
-
-        @pl.when(index == 3)
-        def _():
+        if index == 3:
             finish(y_copy(False))
             ring_z[z] = (ring_y[0] + ring_y[1]) + (ring_y[2] + ring_y[3])
             z_copy(True)
-
-        @pl.when(index == 6)
-        def _():
+        if index == 6:
             finish(z_copy(False))
             cross[core] = ((ring_z[0] + ring_z[1]) + (ring_z[2] + ring_z[3])) + (
                 (ring_z[4] + ring_z[5]) + (ring_z[6] + ring_z[7])
@@ -424,14 +498,12 @@
     w_re, w_im = w[:width], w[width:]
     on_re = halves(w)
     on_im = halves(jnp.concatenate([-w_im, w_re], axis=0))
-    clutter = jnp.zeros((2 * width, length), jnp.float32)
     taps = []
     for half in range(2):
         cut = slice(256 - 128 * half, 256 - 128 * half + length)
-        lags = slice(128 * half, 128 * half + 128)
         taps.append([[table[part, piece, :, cut] for piece in range(2)] for part in range(2)])
-        clutter = clutter + dot3([x[:, lags] for x in on_re], taps[half][0])
-        clutter = clutter + dot3([x[:, lags] for x in on_im], taps[half][1])
+    joined = [[jnp.concatenate([taps[0][part][piece], taps[1][part][piece]], axis=0) for piece in range(2)] for part in range(2)]
+    clutter = dot_stacked(on_re, joined[0]) + dot_stacked(on_im, joined[1])
     residual = jnp.concatenate([surveillance[0], surveillance[1]], axis=0) - clutter
     energy = jnp.sum(residual * residual, axis=1, keepdims=True)
     energy = jnp.broadcast_to(energy[:width] + energy[width:], (width, 128))
@@ -446,7 +518,7 @@
     with_re = halves(jnp.where(own, jnp.concatenate([residual] * segments, axis=0), 0.0))
     with_im = halves(jnp.where(own, jnp.concatenate([swapped] * segments, axis=0), 0.0))
     for half in range(2):
-        block = dot3(taps[half][0], with_re, NT) + dot3(taps[half][1], with_im, NT)
+        block = dot_beside(taps[half][0], with_re) + dot_beside(taps[half][1], with_im)
         corr[16 * half : 16 * half + 16] = block.reshape(16, 8, 128)
 
     to_far = exchange(FAR, lambda p: corr.at[p], lambda p: landed.at[p], far_send, far_recv)
@@ -512,13 +584,14 @@
     return table.astype(np.float32), turns.astype(np.float32)
 
 
-def doppler_kernel(samples, cells, energies, table, turns, out):
+def doppler_kernel(samples, weights, cells, energies, table, turns, out, kept, held, sems):
     near, _, lanes = cells.shape
     groups = near // 2
     segments = turns.shape[1]
     width = lanes // segments // 2
     basis = halves(table[...])
     short = DOPP // segments
+    copies = []
     for g in range(groups):
         power = (energies[g] + energies[groups + g]) / samples
         scale = lax.rsqrt(samples * (power + EPSILON))
@@ -543,32 +616,44 @@
             c, d = turns[0, s : s + 1, :], turns[1, s : s + 1, :]
             total_r = total_r + (y_r * c + y_i * d)
             total_i = total_i + (y_i * c - y_r * d)
-        at = slice(width * g, width * g + width)
-        out[0, 0, at, :] = total_r
-        out[0, 1, at, :] = total_i
-
-
-def doppler(cells, energies, segments, samples):
+        held[g, 0] = total_r
+        held[g, 1] = total_i
+        copy = pltpu.make_async_copy(held.at[g], out.at[0, :, pl.ds(width * g, width), :], sems.at[g])
+        copy.start()
+        copies.append(copy)
+    kept[...] = weights[...]
+    for copy in copies:
+        copy.wait()
+
+
+def doppler(weights, cells, energies, segments, samples):
     vmem = pl.BlockSpec(memory_space=pltpu.VMEM)
     shards = 2 * cells.shape[1]
     table, turns = doppler_tables(shards, segments)
     width = cells.shape[2] // segments // 2
+    groups = cells.shape[0] // 2
     return pl.pallas_call(
         functools.partial(doppler_kernel, samples),
-        out_shape=jax.ShapeDtypeStruct((1, 2, width * cells.shape[0] // 2, DOPP), jnp.float32),
-        in_specs=[vmem] * 4,
-        out_specs=vmem,
+        out_shape=[
+            jax.ShapeDtypeStruct((1, 2, width * groups, DOPP), jnp.float32),
+            jax.ShapeDtypeStruct(weights.shape, jnp.float32),
+        ],
+        in_specs=[vmem] * 5,
+        out_specs=[pl.BlockSpec(memory_space=pl.ANY), vmem],
+        scratch_shapes=[
+            pltpu.VMEM((groups, 2, width, DOPP), jnp.float32),
+            pltpu.SemaphoreType.DMA((groups,)),
+        ],
         name="doppler",
-    )(cells, energies, jnp.asarray(table), jnp.asarray(turns))
+    )(weights, cells, energies, jnp.asarray(table), jnp.asarray(turns))
 
 
 def per_device(reference_signal, surveillance, loading):
     length = reference_signal.shape[1]
-    width = surveillance.shape[1]
     samples = float(length * lax.axis_size(TM))
     weights, cells, energies = cancel(loading, reference_signal, surveillance)
-    full = doppler(cells, energies, length // SEG_LEN, samples)
-    return full, jnp.swapaxes(weights.reshape(2, width, LAGS), 1, 2)
+    full, weights = doppler(weights, cells, energies, length // SEG_LEN, samples)
+    return full, jnp.swapaxes(weights.reshape(2, -1, LAGS), 1, 2)
 
 
 def solution(mesh):

time: 68.2 us -> 70.9 us (1.040)
  Pallas kernels: 66.2 us -> 69.2 us
    pallas_call x1, Pallas kernels: 63.6 us -> 66.2 us  [cancel(): pl.pallas_call(cancel_kernel, out_shape=[jax.ShapeDtypeStruct((2 * width,...]
where the time goes in v3:
time: 70.9 us; the launch traced here: 70.7 us
  Pallas kernels  69.2 us (98%)
  between operations  1.46 us (2%)
    pallas_call x1, Pallas kernels, cancel(): pl.pallas_call(cancel_kernel, out_shape=[jax.ShapeDtypeStruct((2 * width,...  66.2 us
    pallas_call x1, Pallas kernels, doppler(): pl.pallas_call(functools.partial(doppler_kernel, samples), out_shape=[jax...  3.08 us

profile of v3, /device:TPU:1, one launch (start us, length us, event | category | flops | bytes accessed | tf_op | source)
XLA Modules:
  0.0 70.7 jit_solution(5540207027522552795)
XLA Ops:
  1.3 66.2 %cancel.1 = (f32[32,256]{1,0:T(8,128)}, f32[8,32,128]{2,1,0:T(8,128)}, f32[8,8,128]{2,1,0:T(8,128)}) custom-call(f32[1]{0:T(128)S(6)} %copy.7.loading, f32[2,2048]{1,0:T(2,128)} %reference.1, f32[2,16,2048]{2,1,0:T(8,128)} %surveillance.1), custom_call_target="tpu_custom_call" | custom-call | tf_op jit(solution)/shard_map/cancel/pallas_call | solution.py:553
  67.4 3.1 %doppler.1 = (f32[1,2,64,1024]{3,2,1,0:T(8,128)}, f32[32,256]{1,0:T(8,128)}) custom-call(f32[32,256]{1,0:T(8,128)} %get-tuple-element.7.weights, f32[8,32,128]{2,1,0:T(8,128)} %get-tuple-element.8.cells, f32[8,8,128]{2,1,0:T(8,128)} %get-tuple-element.9.energies, f32[64,512]{1,0:T(8,128)} %constant.4.clone.table, f32[2,4,1024]{2,1,0:T(4,128)} %constant.5.clone.turns), custom_call_target="tpu_custom_call" | custom-call | tf_op jit(solution)/shard_map/doppler/pallas_call | solution.py:635

commit v4 on v3

v4 whole, which is shorter than its diff:
```python
import functools

import jax
import jax.numpy as jnp
import numpy as np
from jax import lax
from jax.experimental import pallas as pl
from jax.experimental.pallas import tpu as pltpu
from jax.sharding import Mesh
from jax.sharding import PartitionSpec as P

LAGS = 256
DOPP = 1024
SEG_LEN = 512
TM = ("tm_0", "tm_1", "tm_2")
TM_CHAN = ("tm_0", "tm_1", "tm_2", "chan")
EPSILON = 1e-06
PANEL = 32
UNROLL = 2
PIVOTS = 4
ROWS = 40
MESH = pl.DeviceIdType.MESH

highest = lax.Precision.HIGHEST
NN = (((1,), (0,)), ((), ()))
NT = (((1,), (1,)), ((), ()))


def dot(a, b, dims=NN):
    return lax.dot_general(a, b, dims, precision=highest, preferred_element_type=jnp.float32)


def halves(x):
    high = x.astype(jnp.bfloat16)
    return high, (x - high.astype(jnp.float32)).astype(jnp.bfloat16)


def dot3(a, b, dims=NN):
    def one(x, y):
        return lax.dot_general(x, y, dims, preferred_element_type=jnp.float32)

    return one(a[0], b[0]) + (one(a[0], b[1]) + one(a[1], b[0]))


def dot_beside(a, b):
    both = lax.dot_general(a[0], jnp.concatenate(b, axis=0), NT, preferred_element_type=jnp.float32)
    rest = lax.dot_general(a[1], b[0], NT, preferred_element_type=jnp.float32)
    return both[:, :128] + (both[:, 128:] + rest)


def dot_stacked(a, b):
    rows = a[0].shape[0]
    both = lax.dot_general(jnp.concatenate(a, axis=0), b[0], NN, preferred_element_type=jnp.float32)
    rest = lax.dot_general(a[0], b[1], NN, preferred_element_type=jnp.float32)
    return both[:rows] + (both[rows:] + rest)


def toeplitz(row, rows):
    wide = jnp.broadcast_to(row, (rows, row.shape[1]))
    return pltpu.roll(wide, 0, 1, stride=1, stride_axis=0)


def each(count, act):
    if count == 2:
        act(1)
    else:
        lax.fori_loop(1, count, lambda d, carry: (act(d), carry)[1], 0)


class Exchange:
    def __init__(self, axes, src, dst, send, recv):
        self.axes, self.src, self.dst, self.send, self.recv = axes, src, dst, send, recv
        self.count = int(np.prod([lax.axis_size(a) for a in axes]))

    def copy(self, d):
        here = place(self.axes)
        there = lax.rem(here + d, self.count)
        return pltpu.make_async_remote_copy(
            src_ref=self.src(there),
            dst_ref=self.dst(here),
            send_sem=self.send.at[d - 1],
            recv_sem=self.recv.at[d - 1],
            device_id=device(self.axes, there),
            device_id_type=MESH,
        )

    def start(self):
        each(self.count, lambda d: self.copy(d).start())
        return self

    def wait(self):
        each(self.count, lambda d: self.copy(d).wait())


def place(axes):
    index = lax.axis_index(axes[0])
    for a in axes[1:]:
        index = index * lax.axis_size(a) + lax.axis_index(a)
    return index


def device(axes, index):
    coordinates = {}
    for a in reversed(axes):
        coordinates[a] = lax.rem(index, lax.axis_size(a))
        index = lax.div(index, lax.axis_size(a))
    return coordinates


def greet(barrier, axes, skip=0):
    count = int(np.prod([lax.axis_size(a) for a in axes]))
    here = place(axes)

    def one(d):
        pl.semaphore_signal(
            barrier, inc=1, device_id=device(axes, lax.rem(here + d, count)), device_id_type=MESH
        )

    if skip:
        for d in range(1, count):
            if d != skip:
                one(d)
        return count - 2
    each(count, one)
    return count - 1


def times(a, b):
    if a[1] is None and b[1] is None:
        return (a[0] * b[0], None)
    if a[1] is None:
        return (a[0] * b[0], a[0] * b[1])
    if b[1] is None:
        return (a[0] * b[0], a[1] * b[0])
    return (a[0] * b[0] - a[1] * b[1], a[0] * b[1] + a[1] * b[0])


def plus(a, b):
    if a[1] is None:
        return (a[0] + b[0], b[1])
    if b[1] is None:
        return (a[0] + b[0], a[1])
    return (a[0] + b[0], a[1] + b[1])


def minus(a, b):
    return (a[0] - b[0], None if b[1] is None else a[1] - b[1])


def negative(a):
    return (-a[0], None if a[1] is None else -a[1])


def conjugate(a):
    return (a[0], None if a[1] is None else -a[1])


def product(left, right):
    out = []
    for row in left:
        line = []
        for j in range(len(right[0])):
            total = times(row[0], right[0][j])
            for k in range(1, len(row)):
                total = plus(total, times(row[k], right[k][j]))
            line.append(total)
        out.append(line)
    return out


def adjoint(block):
    return [[conjugate(block[j][i]) for j in range(len(block))] for i in range(len(block[0]))]


def hermitian_inverse(block):
    size = len(block)
    if size == 1:
        return [[(1.0 / block[0][0][0], None)]]
    if size == 2:
        a, c, d = block[0][0][0], block[0][1], block[1][1][0]
        scale = 1.0 / (a * d - (c[0] * c[0] + c[1] * c[1]))
        off = (-c[0] * scale, -c[1] * scale)
        return [[(d * scale, None), off], [conjugate(off), (a * scale, None)]]
    half = size // 2
    head = [row[:half] for row in block[:half]]
    side = [row[half:] for row in block[:half]]
    tail = [row[half:] for row in block[half:]]
    head_inverse = hermitian_inverse(head)
    lifted = product(head_inverse, side)
    drop = product(adjoint(side), lifted)
    rest = [[minus(tail[i][j], drop[i][j]) for j in range(half)] for i in range(half)]
    rest_inverse = hermitian_inverse(rest)
    corner = product(lifted, rest_inverse)
    extra = product(corner, adjoint(lifted))
    first = [[plus(head_inverse[i][j], extra[i][j]) for j in range(half)] for i in range(half)]
    right = [[negative(corner[i][j]) for j in range(half)] for i in range(half)]
    below = adjoint(right)
    return [first[i] + right[i] for i in range(half)] + [below[i] + rest_inverse[i] for i in range(half)]


def added(terms):
    while len(terms) > 1:
        terms = [sum(terms[i : i + 2][1:], terms[i]) for i in range(0, len(terms), 2)]
    return terms[0]


def eliminate(real, imag):
    height, n = real.shape
    m = PIVOTS
    lane = lax.broadcasted_iota(jnp.int32, (1, n), 1)
    lanes = lax.broadcasted_iota(jnp.int32, (height, 128), 1)
    rows = lax.broadcasted_iota(jnp.int32, (height, 128), 0)

    def wide(value):
        return None if value is None else jnp.concatenate([value] * (n // 128), axis=1)

    for k in range(0, height, m):
        col_r = [jnp.broadcast_to(real[:, k + j : k + j + 1], (height, 128)) for j in range(m)]
        col_i = [jnp.broadcast_to(imag[:, k + j : k + j + 1], (height, 128)) for j in range(m)]
        block = [
            [(col_r[j][k + i : k + i + 1], col_i[j][k + i : k + i + 1]) for j in range(m)]
            for i in range(m)
        ]
        inverse = [[(wide(q[0]), wide(q[1])) for q in row] for row in hermitian_inverse(block)]
        hit = (lane >= k) & (lane < k + m)
        old = [
            (
                jnp.where(hit, jnp.where(lane == k + i, 1.0, 0.0), real[k + i : k + i + 1]),
                jnp.where(hit, 0.0, imag[k + i : k + i + 1]),
            )
            for i in range(m)
        ]
        new = product(inverse, [[value] for value in old])
        new = [line[0] for line in new]
        inside = (rows >= k) & (rows < k + m)
        col_r = [jnp.where(inside, jnp.where(rows == k + j, -1.0, 0.0), col_r[j]) for j in range(m)]
        col_i = [jnp.where(inside, 0.0, col_i[j]) for j in range(m)]
        gone = inside | ((lanes >= k) & (lanes < k + m))
        out_r, out_i = [], []
        for t in range(n // 128):
            cut = slice(128 * t, 128 * t + 128)
            mask = gone if t == 0 else inside
            next_r = jnp.where(mask, 0.0, real[:, cut])
            next_i = jnp.where(mask, 0.0, imag[:, cut])
            terms_r, terms_i = [], []
            for j in range(m):
                row_r, row_i = new[j][0][:, cut], new[j][1][:, cut]
                terms_r.append(col_r[j] * row_r - col_i[j] * row_i)
                terms_i.append(col_r[j] * row_i + col_i[j] * row_r)
            out_r.append(next_r - added(terms_r))
            out_i.append(next_i - added(terms_i))
        real = jnp.concatenate(out_r, axis=1)
        imag = jnp.concatenate(out_i, axis=1)
    return real, imag


def thirds(x):
    high = x.astype(jnp.bfloat16)
    rest = x - high.astype(jnp.float32)
    middle = rest.astype(jnp.bfloat16)
    return high, middle, (rest - middle.astype(jnp.float32)).astype(jnp.bfloat16)


def packed(factor, top_r, top_i):
    width = 2 * PANEL
    right = jnp.concatenate(
        [jnp.concatenate([top_r, top_i], axis=1), jnp.concatenate([-top_i, top_r], axis=1)], axis=0
    )
    high, middle, low = thirds(right)
    right = jnp.concatenate([high, middle, low, high, middle, high], axis=0)
    high = factor.astype(jnp.bfloat16).astype(jnp.float32)
    rest = factor - high
    middle = rest.astype(jnp.bfloat16).astype(jnp.float32)
    low = rest - middle
    if width < 128:
        parts = [high + pltpu.roll(high, width, 1), high + pltpu.roll(middle, width, 1), middle + pltpu.roll(low, width, 1)]
    else:
        parts = [high, high, high, middle, middle, low]
    left = jnp.concatenate(parts, axis=1).astype(jnp.bfloat16)
    return lax.dot_general(left, right, NN, preferred_element_type=jnp.float32)


def beside(first, second):
    lane = lax.broadcasted_iota(jnp.int32, first.shape, 1)
    both = jnp.where(lane < PANEL, first, pltpu.roll(second, PANEL, 1))
    return jnp.where(lane < 2 * PANEL, both, 0.0)


def invert(real, imag, top, done, between):
    b = PANEL
    panels = LAGS // b

    def turn(x):
        return pltpu.roll(x, LAGS - b, 1)

    def apply(last, live):
        all_r, all_i = real[...], imag[...]
        row = lax.broadcasted_iota(jnp.int32, (LAGS, 128), 0)
        outside = (row < last * b) | (row >= last * b + b)
        if live is not None:
            outside = outside & live
        factor = jnp.where(outside, beside(all_r[:, :128], all_i[:, :128]), 0.0)
        update = packed(factor, done[0], done[1])
        column = lax.broadcasted_iota(jnp.int32, (LAGS, LAGS), 1)
        drop = column < b
        if live is not None:
            drop = drop & live
        real[...] = turn(jnp.where(drop, 0.0, all_r) - update[:, :LAGS])
        imag[...] = turn(jnp.where(drop, 0.0, all_i) - update[:, LAGS:])
        held = pl.ds(pl.multiple_of(last * b, b), b)
        real[held, :] = turn(done[0])
        imag[held, :] = turn(done[1])

    top[0] = real[:b, :]
    top[1] = imag[:b, :]
    real[...] = pltpu.roll(real[...], b, 1)
    imag[...] = pltpu.roll(imag[...], b, 1)
    done[0] = real[LAGS - b :, :]
    done[1] = imag[LAGS - b :, :]

    def panel(index, carry):
        between(index)
        apply(lax.rem(index + panels - 1, panels), index > 0)
        new_r, new_i = eliminate(top[0], top[1])
        held = pl.ds(pl.multiple_of(lax.rem(index + 1, panels) * b, b), b)
        row_r, row_i = real[held, :], imag[held, :]
        update = packed(beside(row_r[:, :128], row_i[:, :128]), new_r, new_i)
        drop = lax.broadcasted_iota(jnp.int32, (b, LAGS), 1) < b
        top[0] = turn(jnp.where(drop, 0.0, row_r) - update[:, :LAGS])
        top[1] = turn(jnp.where(drop, 0.0, row_i) - update[:, LAGS:])
        done[0] = new_r
        done[1] = new_i
        return carry

    lax.fori_loop(0, panels, panel, 0)
    apply(panels - 1, None)


def edge_matrix(tail):
    blank = jnp.zeros((1, LAGS), jnp.float32)
    edge_r = toeplitz(jnp.concatenate([blank, tail[0:1]], axis=1), LAGS)[:, :LAGS]
    edge_i = toeplitz(jnp.concatenate([blank, tail[1:2]], axis=1), LAGS)[:, :LAGS]
    one = jnp.concatenate([edge_r, edge_i], axis=1)
    two = jnp.concatenate([edge_i, -edge_r], axis=1)
    return dot(one, one, NT), dot(one, two, NT)


def normal_matrix(column, edge_r, edge_i, loading):
    i0 = lax.broadcasted_iota(jnp.int32, (LAGS, LAGS), 0)
    i1 = lax.broadcasted_iota(jnp.int32, (LAGS, LAGS), 1)
    flip = jnp.where(i0 + i1 == LAGS - 1, 1.0, 0.0)
    behind = pltpu.roll(dot(column, flip), 1, 1)
    lane = lax.broadcasted_iota(jnp.int32, behind.shape, 1)
    behind = jnp.where(lane == 0, 0.0, behind)
    base_r = toeplitz(jnp.concatenate([column[0:1], behind[0:1]], axis=1), LAGS)[:, :LAGS]
    base_i = toeplitz(jnp.concatenate([-column[1:2], behind[1:2]], axis=1), LAGS)[:, :LAGS]
    diagonal = i0 == i1
    off = jnp.sum(jnp.sum(jnp.where(diagonal, edge_r, 0.0), axis=0, keepdims=True), axis=1, keepdims=True)
    lam = loading * (column[0:1, 0:1] - off / LAGS)
    real = base_r - edge_r
    return jnp.where(diagonal, real + lam, real), base_i - edge_i


PAIR, FAR, NEAR = TM[2:], TM[:2], (TM[2], "chan")
ALONG_Y, ALONG_Z = TM[:1], TM[1:2]


def cancel_kernel(
    loading, reference, surveillance, weights, cells, energies,
    table, halo, tail, mine, gram_pair, gram_all, real, imag, top, done,
    pair, ring_y, ring_z, cross, residual, corr, landed, turned, power, power_z, power_y,
    edge_sem, tail_send, tail_recv, gram_sem, gram_send, gram_recv,
    pair_sem, y_send, y_recv, z_send, z_recv, out_sem,
    far_send, far_recv, near_send, near_recv, pz_send, pz_recv, py_send, py_recv, pa_send, pa_recv,
):
    length = reference.shape[1]
    width = surveillance.shape[1]
    count = lax.axis_size(TM)
    here = place(TM)
    core, y, z, far, near = place(PAIR), place(ALONG_Y), place(ALONG_Z), place(FAR), place(NEAR)
    barrier = pltpu.get_barrier_semaphore()
    total = greet(barrier, TM)
    total += greet(barrier, NEAR, 4)

    def fill(tile, windows):
        delayed = [toeplitz(x, 128)[:, 128:] for x in windows]
        at = pl.ds(pl.multiple_of(128 * tile, 128), 128)
        for part in range(2):
            high, low = halves(delayed[part])
            table[part, 0, :, at] = high
            table[part, 1, :, at] = low
        return delayed

    def lagged(delayed, start):
        now = reference[:, pl.ds(pl.multiple_of(start, 128), 128)]
        now_r, now_i = now[0:1], now[1:2]
        return (delayed[0] * now_r + delayed[1] * now_i, delayed[0] * now_i - delayed[1] * now_r)

    def plus_all(sums, terms):
        return tuple(x + y for x, y in zip(sums, terms))

    tiles = (LAGS + length) // 128

    def fill_inner(tile, sums):
        start = pl.multiple_of(128 * tile - 384, 128)
        window = reference[:, pl.ds(start, LAGS)]
        delayed = fill(tile, [window[0:1], window[1:2]])
        return (
            plus_all(sums[0], lagged(delayed, 128 * tile - 256)),
            plus_all(sums[1], lagged(delayed, 128 * tile - 128)),
        )

    blank = (jnp.zeros((128, 128), jnp.float32),) * 2
    sums = lax.fori_loop(3, tiles - 1, fill_inner, (blank, blank))
    window = reference[:, length - LAGS :]
    delayed = fill(tiles - 1, [window[0:1], window[1:2]])
    sums = [plus_all(sums[0], lagged(delayed, length - 128)), sums[1]]

    pl.semaphore_wait(barrier, total)
    forward = pltpu.make_async_remote_copy(
        src_ref=reference.at[:, pl.ds(length - LAGS, LAGS)],
        dst_ref=halo,
        send_sem=edge_sem.at[0],
        recv_sem=edge_sem.at[1],
        device_id=device(TM, lax.rem(here + 1, count)),
        device_id_type=MESH,
    )
    forward.start()

    def tail_copy(d):
        return pltpu.make_async_remote_copy(
            src_ref=reference.at[:, pl.ds(length - LAGS, LAGS)],
            dst_ref=tail,
            send_sem=tail_send.at[d - 1],
            recv_sem=tail_recv.at[0],
            device_id=device(TM, lax.rem(here + d, count)),
            device_id_type=MESH,
        )

    @pl.when(here == count - 1)
    def _():
        tail[...] = reference[:, length - LAGS :]
        each(count, lambda d: tail_copy(d).start())

    forward.wait()
    before = jnp.where(here > 0, halo[...], 0.0)
    delayed = fill(1, [before[0:1], before[1:2]])
    sums[1] = plus_all(sums[1], lagged(delayed, 0))
    joint = jnp.concatenate([before[:, 128:], reference[:, :128]], axis=1)
    delayed = fill(2, [joint[0:1], joint[1:2]])
    sums[0] = plus_all(sums[0], lagged(delayed, 0))
    sums[1] = plus_all(sums[1], lagged(delayed, 128))
    for half in range(2):
        for part in range(2):
            line = jnp.sum(sums[half][part].T, axis=0, keepdims=True)
            gram_pair[0, 2 * part + half : 2 * part + half + 1, :] = line
    Exchange(PAIR, lambda p: gram_pair.at[0], lambda p: gram_pair.at[1], gram_sem.at[0:1], gram_sem.at[1:2]).start().wait()
    gram_all[far] = gram_pair[0] + gram_pair[1]
    to_gram = Exchange(FAR, lambda p: gram_all.at[far], lambda p: gram_all.at[p], gram_send, gram_recv).start()

    segments = length // SEG_LEN

    def taps_of(segment):
        taps = []
        for half in range(2):
            at = pl.ds(pl.multiple_of(segment * SEG_LEN + 256 - 128 * half, 128), SEG_LEN)
            taps.append([[table[part, piece, :, at] for piece in range(2)] for part in range(2)])
        return taps

    def signal_of(segment):
        at = pl.ds(pl.multiple_of(segment * SEG_LEN, 128), SEG_LEN)
        return surveillance[0, :, at], surveillance[1, :, at]

    def cross_terms(segment, total):
        s_re, s_im = signal_of(segment)
        zero = jnp.zeros((128 - 2 * width, SEG_LEN), jnp.float32)
        with_re = halves(jnp.concatenate([s_re, s_im, zero], axis=0))
        with_im = halves(jnp.concatenate([s_im, -s_re, zero], axis=0))
        return tuple(
            x + (dot_beside(taps[0], with_re) + dot_beside(taps[1], with_im))
            for x, taps in zip(total, taps_of(segment))
        )

    product = lax.fori_loop(0, segments, cross_terms, blank, unroll=UNROLL)
    for half in range(2):
        mine[half] = product[half].T[: 2 * width]
    to_pair = Exchange(PAIR, lambda p: mine.at[p], lambda p: pair, pair_sem.at[0:1], pair_sem.at[1:2]).start()

    @pl.when(here == count - 1)
    def _():
        each(count, lambda d: tail_copy(d).wait_send())

    @pl.when(here != count - 1)
    def _():
        tail_copy(1).wait_recv()

    edge_r, edge_i = edge_matrix(tail[...])
    real[...] = edge_r
    imag[...] = edge_i
    to_gram.wait()
    gram = jnp.sum(gram_all[...], axis=0)
    column = jnp.concatenate([gram[0:1], gram[1:2]], axis=1)
    column = jnp.concatenate([column, jnp.concatenate([gram[2:3], gram[3:4]], axis=1)], axis=0)
    column = jnp.concatenate([column, jnp.zeros((6, LAGS), jnp.float32)], axis=0)
    start_r, start_i = normal_matrix(column, real[...], imag[...], loading[0])
    real[...] = start_r
    imag[...] = start_i

    along_y = Exchange(ALONG_Y, lambda p: ring_y.at[y], lambda p: ring_y.at[p], y_send, y_recv)
    along_z = Exchange(ALONG_Z, lambda p: ring_z.at[z], lambda p: ring_z.at[p], z_send, z_recv)
    out = Exchange(PAIR, lambda p: cross.at[core], lambda p: cross.at[p], out_sem.at[0:1], out_sem.at[1:2])

    def between(index):
        @pl.when(index == 1)
        def _():
            to_pair.wait()
            ring_y[y] = mine[core] + pair[...]
            along_y.start()

        @pl.when(index == 3)
        def _():
            along_y.wait()
            ring_z[z] = (ring_y[0] + ring_y[1]) + (ring_y[2] + ring_y[3])
            along_z.start()

        @pl.when(index == 6)
        def _():
            along_z.wait()
            cross[core] = ((ring_z[0] + ring_z[1]) + (ring_z[2] + ring_z[3])) + (
                (ring_z[4] + ring_z[5]) + (ring_z[6] + ring_z[7])
            )
            out.start()

    invert(real, imag, top, done, between)
    out.wait()
    right = jnp.concatenate([cross[0], cross[1]], axis=1)
    spun = jnp.concatenate([-right[width:], right[:width]], axis=0)
    w = dot(right, real[...], NT) + dot(spun, imag[...], NT)
    weights[...] = w

    w_re, w_im = w[:width], w[width:]
    on_re = halves(w)
    on_im = halves(jnp.concatenate([-w_im, w_re], axis=0))
    own_row = lax.broadcasted_iota(jnp.int32, (128, SEG_LEN), 0) // (2 * width)

    def cancelled(segment, energy):
        taps = taps_of(segment)
        joined = [
            [jnp.concatenate([taps[0][part][piece], taps[1][part][piece]], axis=0) for piece in range(2)]
            for part in range(2)
        ]
        clutter = dot_stacked(on_re, joined[0]) + dot_stacked(on_im, joined[1])
        rest = jnp.concatenate(signal_of(segment), axis=0) - clutter
        residual[segment] = rest
        square = rest * rest
        for tile in range(SEG_LEN // 128):
            energy = energy + square[:, 128 * tile : 128 * tile + 128]
        return energy

    energy = lax.fori_loop(0, segments, cancelled, jnp.zeros((2 * width, 128), jnp.float32), unroll=UNROLL)
    energy = jnp.sum(energy, axis=1, keepdims=True)
    energy = jnp.broadcast_to(energy[:width] + energy[width:], (width, 128))
    energy = jnp.concatenate([energy, jnp.zeros((128 - width, 128), jnp.float32)], axis=0)
    power_z[z] = energy.T[:8]
    to_z = Exchange(ALONG_Z, lambda p: power_z.at[z], lambda p: power_z.at[p], pz_send, pz_recv).start()

    to_far = Exchange(FAR, lambda p: corr.at[p], lambda p: landed.at[p], far_send, far_recv)
    for half in range(2):

        def correlate(segment, total):
            at = pl.ds(pl.multiple_of(segment * SEG_LEN + 256 - 128 * half, 128), SEG_LEN)
            rest = residual[segment]
            swapped = jnp.concatenate([rest[width:], -rest[:width]], axis=0)
            own = own_row == segment
            with_re = halves(jnp.where(own, jnp.concatenate([rest] * segments, axis=0), 0.0))
            with_im = halves(jnp.where(own, jnp.concatenate([swapped] * segments, axis=0), 0.0))
            real_taps = [table[0, piece, :, at] for piece in range(2)]
            imag_taps = [table[1, piece, :, at] for piece in range(2)]
            return total + (dot_beside(real_taps, with_re) + dot_beside(imag_taps, with_im))

        total = lax.fori_loop(0, segments, correlate, blank[0], unroll=UNROLL)
        corr[16 * half : 16 * half + 16] = total.reshape(16, 8, 128)

        def send(p, carry):
            @pl.when(p != far)
            def _():
                to_far.copy(lax.rem(p - far + 32, 32)).start()

            return carry

        lax.fori_loop(16 * half, 16 * half + 16, send, 0)
    landed[far] = corr[far]
    to_z.wait()
    parts = [power_z[i] for i in range(8)]
    power_y[y] = ((parts[0] + parts[1]) + (parts[2] + parts[3])) + ((parts[4] + parts[5]) + (parts[6] + parts[7]))
    to_y = Exchange(ALONG_Y, lambda p: power_y.at[y], lambda p: power_y.at[p], py_send, py_recv).start()
    to_far.wait()
    everything = landed[...]
    for lag in range(8):
        turned[lag] = everything[:, lag, :]
    to_near = Exchange(NEAR, lambda p: turned.at[p], lambda p: cells.at[p], near_send, near_recv).start()
    cells[near] = turned[near]
    to_y.wait()
    power[...] = (power_y[0] + power_y[1]) + (power_y[2] + power_y[3])
    energies[near] = power[...]
    Exchange(NEAR, lambda p: power, lambda p: energies.at[p], pa_send, pa_recv).start().wait()
    to_near.wait()


def cancel(loading, reference, surveillance):
    vmem = pl.BlockSpec(memory_space=pltpu.VMEM)
    length = reference.shape[1]
    width = surveillance.shape[1]
    dma = pltpu.SemaphoreType.DMA

    def block(*shape):
        return pltpu.VMEM(shape, jnp.float32)

    half = (2 * width, 128)
    return pl.pallas_call(
        cancel_kernel,
        out_shape=[
            jax.ShapeDtypeStruct((2 * width, LAGS), jnp.float32),
            jax.ShapeDtypeStruct((8, 32, 128), jnp.float32),
            jax.ShapeDtypeStruct((8, 8, 128), jnp.float32),
        ],
        in_specs=[pl.BlockSpec(memory_space=pltpu.SMEM), vmem, vmem],
        out_specs=[vmem] * 3,
        scratch_shapes=[
            pltpu.VMEM((2, 2, 128, LAGS + length), jnp.bfloat16),
            block(2, LAGS), block(2, LAGS), block(2, *half), block(2, 4, 128), block(32, 4, 128),
            block(LAGS, LAGS), block(LAGS, LAGS), block(2, PANEL, LAGS), block(2, PANEL, LAGS),
            block(*half), block(4, *half), block(8, *half), block(2, *half), block(4, 2 * width, SEG_LEN),
            block(32, 8, 128), block(32, 8, 128), block(8, 32, 128), block(8, 128), block(8, 8, 128), block(4, 8, 128),
            dma((2,)), dma((63,)), dma((1,)), dma((2,)), dma((31,)), dma((31,)),
            dma((2,)), dma((3,)), dma((3,)), dma((7,)), dma((7,)), dma((2,)),
            dma((31,)), dma((31,)), dma((7,)), dma((7,)), dma((7,)), dma((7,)), dma((3,)), dma((3,)), dma((7,)), dma((7,)),
        ],
        compiler_params=pltpu.CompilerParams(collective_id=0, has_side_effects=True, vmem_limit_bytes=24 * 2**20),
        name="cancel",
    )(loading, reference, surveillance)


def doppler_tables(shards, segments):
    short = DOPP // segments
    order = np.arange(shards).reshape(-1, 2).T.reshape(-1)
    angle = 2.0 * np.pi / short * (np.outer(order, np.arange(short)) % short)
    table = np.concatenate([np.cos(angle), np.sin(angle)], axis=1)
    turn = 2.0 * np.pi / DOPP * np.outer(np.arange(segments), np.arange(DOPP))
    turns = np.stack([np.cos(turn), np.sin(turn)])
    return table.astype(np.float32), turns.astype(np.float32)


def doppler_kernel(samples, weights, cells, energies, table, turns, out, kept):
    near, _, lanes = cells.shape
    groups = near // 2
    segments = turns.shape[1]
    width = lanes // segments // 2
    basis = halves(table[...])
    short = DOPP // segments
    def group(g, carry):
        power = (energies[g] + energies[groups + g]) / samples
        scale = lax.rsqrt(samples * (power + EPSILON))
        by = jnp.broadcast_to(scale[0:1], (128, 128)).T[:width, 0:1]
        rows = jnp.concatenate([cells[g], cells[groups + g]], axis=0)
        wave = dot3(halves(rows.T), basis)
        total_r = total_i = None
        for s in range(segments):
            base = 2 * width * s
            a_r, a_i = wave[base : base + width, :short], wave[base : base + width, short:]
            b_r, b_i = (
                wave[base + width : base + 2 * width, :short],
                wave[base + width : base + 2 * width, short:],
            )
            y_r = (a_r + b_i) * by
            y_i = (b_r - a_i) * by
            y_r = jnp.concatenate([y_r] * segments, axis=1)
            y_i = jnp.concatenate([y_i] * segments, axis=1)
            if s == 0:
                total_r, total_i = y_r, y_i
                continue
            c, d = turns[0, s : s + 1, :], turns[1, s : s + 1, :]
            total_r = total_r + (y_r * c + y_i * d)
            total_i = total_i + (y_i * c - y_r * d)
        at = pl.ds(width * g, width)
        out[0, 0, at, :] = total_r
        out[0, 1, at, :] = total_i
        return carry

    for g in range(groups):
        group(g, 0)
    kept[...] = weights[...]


def doppler(weights, cells, energies, segments, samples):
    vmem = pl.BlockSpec(memory_space=pltpu.VMEM)
    shards = 2 * cells.shape[1]
    table, turns = doppler_tables(shards, segments)
    width = cells.shape[2] // segments // 2
    groups = cells.shape[0] // 2
    return pl.pallas_call(
        functools.partial(doppler_kernel, samples),
        out_shape=[
            jax.ShapeDtypeStruct((1, 2, width * groups, DOPP), jnp.float32),
            jax.ShapeDtypeStruct(weights.shape, jnp.float32),
        ],
        in_specs=[vmem] * 5,
        out_specs=[vmem, vmem],
        compiler_params=pltpu.CompilerParams(vmem_limit_bytes=24 * 2**20),
        name="doppler",
    )(weights, cells, energies, jnp.asarray(table), jnp.asarray(turns))


def per_device(reference_signal, surveillance, loading):
    length = reference_signal.shape[1]
    samples = float(length * lax.axis_size(TM))
    weights, cells, energies = cancel(loading, reference_signal, surveillance)
    full, weights = doppler(weights, cells, energies, length // SEG_LEN, samples)
    return full, jnp.swapaxes(weights.reshape(2, -1, LAGS), 1, 2)


def solution(mesh):
    split = Mesh(
        mesh.devices.reshape(4, 8, 2, mesh.shape["chan"]), ("tm_0", "tm_1", "tm_2", "chan")
    )
    in_specs = (P(None, TM), P(None, "chan", TM), P())
    out_specs = (P(TM_CHAN, None, None, None), P(None, None, "chan"))
    return jax.shard_map(
        per_device, mesh=split, in_specs=in_specs, out_specs=out_specs, check_vma=False
    )
```

time: 70.9 us -> 60.1 us (0.85)
  Pallas kernels: 69.2 us -> 57 us
  local copies, waits for them, and re-layouts: 0 us -> 1.67 us
    pallas_call x1, Pallas kernels: 66.2 us -> 55.4 us  [cancel(): pl.pallas_call(cancel_kernel, out_shape=[jax.ShapeDtypeStruct((2 * width,...]
    unnamed x0 -> x8, local copies, waits for them, and re-layouts: none -> 1.67 us
    pallas_call x1, Pallas kernels: 3.08 us -> 1.57 us  [doppler(): pl.pallas_call(functools.partial(doppler_kernel, samples), out_shape=[jax...]
where the time goes in v4:
time: 60.1 us; the launch traced here: 60 us
  Pallas kernels  57 us (95%)
  local copies, waits for them, and re-layouts  1.67 us (3%)
  between operations  1.31 us (2%)
    pallas_call x1, Pallas kernels, cancel(): pl.pallas_call(cancel_kernel, out_shape=[jax.ShapeDtypeStruct((2 * width,...  55.4 us
    unnamed x8, local copies, waits for them, and re-layouts  1.67 us
    pallas_call x1, Pallas kernels, doppler(): pl.pallas_call(functools.partial(doppler_kernel, samples), out_shape=[jax...  1.57 us

profile of v4, /device:TPU:1, one launch (start us, length us, event | category | flops | bytes accessed | tf_op | source)
XLA Modules:
  0.0 60.0 jit_solution(41241812547329062)
XLA Ops:
  1.3 0.0 copy-start
  1.3 0.9 %copy-done = f32[2,16,2048]{2,1,0:T(8,128)S(1)} copy-done((f32[2,16,2048]{2,1,0:T(8,128)S(1)}, f32[2,16,2048]{2,1,0:T(8,128)}, u32[]{:S(2)}) %copy-start) | copy-done | bytes 262168
  2.2 0.0 copy-start.3
  2.2 0.7 %copy-done.3 = f32[2,2048]{1,0:T(2,128)S(1)} copy-done((f32[2,2048]{1,0:T(2,128)S(1)}, f32[2,2048]{1,0:T(2,128)}, u32[]{:S(2)}) %copy-start.3) | copy-done | bytes 16408
  2.9 0.0 copy-start.1
  2.9 0.0 copy-start.2
  2.9 55.4 %cancel.1 = (f32[32,256]{1,0:T(8,128)S(1)}, f32[8,32,128]{2,1,0:T(8,128)S(1)}, f32[8,8,128]{2,1,0:T(8,128)S(1)}) custom-call(f32[1]{0:T(128)S(6)} %copy.7.loading, f32[2,2048]{1,0:T(2,128)S(1)} %copy-done.3, f32[2,16,2048]{2,1,0:T(8,128)S(1)} %copy-done), custom_call_target="tpu_custom_call" | custom-call | tf_op jit(solution)/shard_map/cancel/pallas_call | solution.py:620
  58.4 0.0 copy-done.1
  58.4 0.0 copy-done.2
  58.4 1.6 %doppler.1 = (f32[1,2,64,1024]{3,2,1,0:T(8,128)}, f32[32,256]{1,0:T(8,128)}) custom-call(f32[32,256]{1,0:T(8,128)S(1)} %get-tuple-element.7.weights, f32[8,32,128]{2,1,0:T(8,128)S(1)} %get-tuple-element.8.cells, f32[8,8,128]{2,1,0:T(8,128)S(1)} %get-tuple-element.9.energies, f32[64,512]{1,0:T(8,128)S(1)} %copy-done.1, f32[2,4,1024]{2,1,0:T(4,128)S(1)} %copy-done.2), custom_call_target="tpu_custom_call" | custom-call | tf_op jit(solution)/shard_map/doppler/pallas_call | solution.py:701
Async XLA Ops:
  1.3 1.0 %copy-start = (f32[2,16,2048]{2,1,0:T(8,128)S(1)}, f32[2,16,2048]{2,1,0:T(8,128)}, u32[]{:S(2)}) copy-start(f32[2,16,2048]{2,1,0:T(8,128)} %surveillance.1) | copy-start | bytes 786436
  2.2 0.7 %copy-start.3 = (f32[2,2048]{1,0:T(2,128)S(1)}, f32[2,2048]{1,0:T(2,128)}, u32[]{:S(2)}) copy-start(f32[2,2048]{1,0:T(2,128)} %reference.1) | copy-start | bytes 49156
  2.9 55.4 %copy-start.1 = (f32[64,512]{1,0:T(8,128)S(1)}, f32[64,512]{1,0:T(8,128)}, u32[]{:S(2)}) copy-start(f32[64,512]{1,0:T(8,128)} %constant.4.clone.table) | copy-start | bytes 393220
  2.9 55.4 %copy-start.2 = (f32[2,4,1024]{2,1,0:T(4,128)S(1)}, f32[2,4,1024]{2,1,0:T(4,128)}, u32[]{:S(2)}) copy-start(f32[2,4,1024]{2,1,0:T(4,128)} %constant.5.clone.turns) | copy-start | bytes 98308

commit v5 on v4

--- a/solution.py
+++ b/solution.py
@@ -366,8 +366,8 @@
 
 
 def cancel_kernel(
-    loading, reference, surveillance, weights, cells, energies,
-    table, halo, tail, mine, gram_pair, gram_all, real, imag, top, done,
+    loading, reference_hbm, surveillance_hbm, weights, cells, energies,
+    reference, surveillance, fetch_sem, table, halo, tail, mine, gram_pair, gram_all, real, imag, top, done,
     pair, ring_y, ring_z, cross, residual, corr, landed, turned, power, power_z, power_y,
     edge_sem, tail_send, tail_recv, gram_sem, gram_send, gram_recv,
     pair_sem, y_send, y_recv, z_send, z_recv, out_sem,
@@ -378,9 +378,14 @@
     count = lax.axis_size(TM)
     here = place(TM)
     core, y, z, far, near = place(PAIR), place(ALONG_Y), place(ALONG_Z), place(FAR), place(NEAR)
+    fetch_r = pltpu.make_async_copy(reference_hbm, reference, fetch_sem.at[0])
+    fetch_r.start()
+    fetch_s = pltpu.make_async_copy(surveillance_hbm, surveillance, fetch_sem.at[1])
+    fetch_s.start()
     barrier = pltpu.get_barrier_semaphore()
     total = greet(barrier, TM)
     total += greet(barrier, NEAR, 4)
+    fetch_r.wait()
 
     def fill(tile, windows):
         delayed = [toeplitz(x, 128)[:, 128:] for x in windows]
@@ -458,6 +463,7 @@
     gram_all[far] = gram_pair[0] + gram_pair[1]
     to_gram = Exchange(FAR, lambda p: gram_all.at[far], lambda p: gram_all.at[p], gram_send, gram_recv).start()
 
+    fetch_s.wait()
     segments = length // SEG_LEN
 
     def taps_of(segment):
@@ -497,6 +503,10 @@
     edge_r, edge_i = edge_matrix(tail[...])
     real[...] = edge_r
     imag[...] = edge_i
+    along_y = Exchange(ALONG_Y, lambda p: ring_y.at[y], lambda p: ring_y.at[p], y_send, y_recv)
+    to_pair.wait()
+    ring_y[y] = mine[core] + pair[...]
+    along_y.start()
     to_gram.wait()
     gram = jnp.sum(gram_all[...], axis=0)
     column = jnp.concatenate([gram[0:1], gram[1:2]], axis=1)
@@ -506,18 +516,11 @@
     real[...] = start_r
     imag[...] = start_i
 
-    along_y = Exchange(ALONG_Y, lambda p: ring_y.at[y], lambda p: ring_y.at[p], y_send, y_recv)
     along_z = Exchange(ALONG_Z, lambda p: ring_z.at[z], lambda p: ring_z.at[p], z_send, z_recv)
     out = Exchange(PAIR, lambda p: cross.at[core], lambda p: cross.at[p], out_sem.at[0:1], out_sem.at[1:2])
 
     def between(index):
-        @pl.when(index == 1)
-        def _():
-            to_pair.wait()
-            ring_y[y] = mine[core] + pair[...]
-            along_y.start()
-
-        @pl.when(index == 3)
+        @pl.when(index == 2)
         def _():
             along_y.wait()
             ring_z[z] = (ring_y[0] + ring_y[1]) + (ring_y[2] + ring_y[3])
@@ -624,9 +627,10 @@
             jax.ShapeDtypeStruct((8, 32, 128), jnp.float32),
             jax.ShapeDtypeStruct((8, 8, 128), jnp.float32),
         ],
-        in_specs=[pl.BlockSpec(memory_space=pltpu.SMEM), vmem, vmem],
+        in_specs=[pl.BlockSpec(memory_space=pltpu.SMEM)] + [pl.BlockSpec(memory_space=pltpu.HBM)] * 2,
         out_specs=[vmem] * 3,
         scratch_shapes=[
+            block(*reference.shape), block(*surveillance.shape), dma((2,)),
             pltpu.VMEM((2, 2, 128, LAGS + length), jnp.bfloat16),
             block(2, LAGS), block(2, LAGS), block(2, *half), block(2, 4, 128), block(32, 4, 128),
             block(LAGS, LAGS), block(LAGS, LAGS), block(2, PANEL, LAGS), block(2, PANEL, LAGS),

time: 60.1 us -> 60.3 us (level)
  no operation moved by 1% of the time
where the time goes in v5:
time: 60.3 us; the launch traced here: 60.2 us
  Pallas kernels  57.2 us (95%)
  local copies, waits for them, and re-layouts  1.67 us (3%)
  between operations  1.31 us (2%)
    pallas_call x1, Pallas kernels, cancel(): pl.pallas_call(cancel_kernel, out_shape=[jax.ShapeDtypeStruct((2 * width,...  55.6 us
    unnamed x8, local copies, waits for them, and re-layouts  1.67 us
    pallas_call x1, Pallas kernels, doppler(): pl.pallas_call(functools.partial(doppler_kernel, samples), out_shape=[jax...  1.57 us

profile of v5, /device:TPU:1, one launch (start us, length us, event | category | flops | bytes accessed | tf_op | source)
XLA Modules:
  0.0 60.2 jit_solution(10135575241948783337)
XLA Ops:
  1.3 0.0 copy-start
  1.3 0.9 %copy-done = f32[2,16,2048]{2,1,0:T(8,128)S(1)} copy-done((f32[2,16,2048]{2,1,0:T(8,128)S(1)}, f32[2,16,2048]{2,1,0:T(8,128)}, u32[]{:S(2)}) %copy-start) | copy-done | bytes 262168
  2.2 0.0 copy-start.3
  2.2 0.7 %copy-done.3 = f32[2,2048]{1,0:T(2,128)S(1)} copy-done((f32[2,2048]{1,0:T(2,128)S(1)}, f32[2,2048]{1,0:T(2,128)}, u32[]{:S(2)}) %copy-start.3) | copy-done | bytes 16408
  2.9 0.0 copy-start.1
  2.9 0.0 copy-start.2
  2.9 55.6 %cancel.1 = (f32[32,256]{1,0:T(8,128)S(1)}, f32[8,32,128]{2,1,0:T(8,128)S(1)}, f32[8,8,128]{2,1,0:T(8,128)S(1)}) custom-call(f32[1]{0:T(128)S(6)} %copy.7.loading, f32[2,2048]{1,0:T(2,128)S(1)} %copy-done.3, f32[2,16,2048]{2,1,0:T(8,128)S(1)} %copy-done), custom_call_target="tpu_custom_call" | custom-call | tf_op jit(solution)/shard_map/cancel/pallas_call | solution.py:623
  58.6 0.0 copy-done.1
  58.6 0.0 copy-done.2
  58.6 1.6 %doppler.1 = (f32[1,2,64,1024]{3,2,1,0:T(8,128)}, f32[32,256]{1,0:T(8,128)}) custom-call(f32[32,256]{1,0:T(8,128)S(1)} %get-tuple-element.7.weights, f32[8,32,128]{2,1,0:T(8,128)S(1)} %get-tuple-element.8.cells, f32[8,8,128]{2,1,0:T(8,128)S(1)} %get-tuple-element.9.energies, f32[64,512]{1,0:T(8,128)S(1)} %copy-done.1, f32[2,4,1024]{2,1,0:T(4,128)S(1)} %copy-done.2), custom_call_target="tpu_custom_call" | custom-call | tf_op jit(solution)/shard_map/doppler/pallas_call | solution.py:705
Async XLA Ops:
  1.3 1.0 %copy-start = (f32[2,16,2048]{2,1,0:T(8,128)S(1)}, f32[2,16,2048]{2,1,0:T(8,128)}, u32[]{:S(2)}) copy-start(f32[2,16,2048]{2,1,0:T(8,128)} %surveillance_hbm.1) | copy-start | bytes 786436
  2.2 0.7 %copy-start.3 = (f32[2,2048]{1,0:T(2,128)S(1)}, f32[2,2048]{1,0:T(2,128)}, u32[]{:S(2)}) copy-start(f32[2,2048]{1,0:T(2,128)} %reference_hbm.1) | copy-start | bytes 49156
  2.9 55.6 %copy-start.1 = (f32[64,512]{1,0:T(8,128)S(1)}, f32[64,512]{1,0:T(8,128)}, u32[]{:S(2)}) copy-start(f32[64,512]{1,0:T(8,128)} %constant.4.clone.table) | copy-start | bytes 393220
  2.9 55.6 %copy-start.2 = (f32[2,4,1024]{2,1,0:T(4,128)S(1)}, f32[2,4,1024]{2,1,0:T(4,128)}, u32[]{:S(2)}) copy-start(f32[2,4,1024]{2,1,0:T(4,128)} %constant.5.clone.turns) | copy-start | bytes 98308

commit v6 on v4

--- a/solution.py
+++ b/solution.py
@@ -368,10 +368,10 @@
 def cancel_kernel(
     loading, reference, surveillance, weights, cells, energies,
     table, halo, tail, mine, gram_pair, gram_all, real, imag, top, done,
-    pair, ring_y, ring_z, cross, residual, corr, landed, turned, power, power_z, power_y,
+    pair, ring_y, ring_z, cross, residual, corr, power, power_far,
     edge_sem, tail_send, tail_recv, gram_sem, gram_send, gram_recv,
     pair_sem, y_send, y_recv, z_send, z_recv, out_sem,
-    far_send, far_recv, near_send, near_recv, pz_send, pz_recv, py_send, py_recv, pa_send, pa_recv,
+    all_send, all_recv, pf_send, pf_recv, pn_send, pn_recv,
 ):
     length = reference.shape[1]
     width = surveillance.shape[1]
@@ -561,10 +561,12 @@
     energy = jnp.sum(energy, axis=1, keepdims=True)
     energy = jnp.broadcast_to(energy[:width] + energy[width:], (width, 128))
     energy = jnp.concatenate([energy, jnp.zeros((128 - width, 128), jnp.float32)], axis=0)
-    power_z[z] = energy.T[:8]
-    to_z = Exchange(ALONG_Z, lambda p: power_z.at[z], lambda p: power_z.at[p], pz_send, pz_recv).start()
-
-    to_far = Exchange(FAR, lambda p: corr.at[p], lambda p: landed.at[p], far_send, far_recv)
+    power_far[far] = energy.T[:1]
+    to_power = Exchange(FAR, lambda p: power_far.at[far], lambda p: power_far.at[p], pf_send, pf_recv).start()
+
+    me = place(TM_CHAN)
+    slot = lax.axis_index("chan") * count + here
+    to_all = Exchange(TM_CHAN, lambda p: corr.at[p], lambda p: cells.at[slot], all_send, all_recv)
     for half in range(2):
 
         def correlate(segment, total):
@@ -579,31 +581,24 @@
             return total + (dot_beside(real_taps, with_re) + dot_beside(imag_taps, with_im))
 
         total = lax.fori_loop(0, segments, correlate, blank[0], unroll=UNROLL)
-        corr[16 * half : 16 * half + 16] = total.reshape(16, 8, 128)
-
-        def send(p, carry):
-            @pl.when(p != far)
+        corr[128 * half : 128 * half + 128] = total.reshape(128, 1, 128)
+
+        def send(i, carry):
+            p = 128 * half + lax.rem(me + i, 128)
+
+            @pl.when(p != me)
             def _():
-                to_far.copy(lax.rem(p - far + 32, 32)).start()
+                to_all.copy(lax.rem(p - me + LAGS, LAGS)).start()
 
             return carry
 
-        lax.fori_loop(16 * half, 16 * half + 16, send, 0)
-    landed[far] = corr[far]
-    to_z.wait()
-    parts = [power_z[i] for i in range(8)]
-    power_y[y] = ((parts[0] + parts[1]) + (parts[2] + parts[3])) + ((parts[4] + parts[5]) + (parts[6] + parts[7]))
-    to_y = Exchange(ALONG_Y, lambda p: power_y.at[y], lambda p: power_y.at[p], py_send, py_recv).start()
-    to_far.wait()
-    everything = landed[...]
-    for lag in range(8):
-        turned[lag] = everything[:, lag, :]
-    to_near = Exchange(NEAR, lambda p: turned.at[p], lambda p: cells.at[p], near_send, near_recv).start()
-    cells[near] = turned[near]
-    to_y.wait()
-    power[...] = (power_y[0] + power_y[1]) + (power_y[2] + power_y[3])
+        lax.fori_loop(0, 128, send, 0)
+    cells[slot] = corr[me]
+    to_power.wait()
+    power[...] = jnp.sum(power_far[...], axis=0)
     energies[near] = power[...]
-    Exchange(NEAR, lambda p: power, lambda p: energies.at[p], pa_send, pa_recv).start().wait()
+    to_near = Exchange(NEAR, lambda p: power, lambda p: energies.at[p], pn_send, pn_recv).start()
+    to_all.wait()
     to_near.wait()
 
 
@@ -621,8 +616,8 @@
         cancel_kernel,
         out_shape=[
             jax.ShapeDtypeStruct((2 * width, LAGS), jnp.float32),
-            jax.ShapeDtypeStruct((8, 32, 128), jnp.float32),
-            jax.ShapeDtypeStruct((8, 8, 128), jnp.float32),
+            jax.ShapeDtypeStruct((LAGS, 1, 128), jnp.float32),
+            jax.ShapeDtypeStruct((8, 1, 128), jnp.float32),
         ],
         in_specs=[pl.BlockSpec(memory_space=pltpu.SMEM), vmem, vmem],
         out_specs=[vmem] * 3,
@@ -631,10 +626,10 @@
             block(2, LAGS), block(2, LAGS), block(2, *half), block(2, 4, 128), block(32, 4, 128),
             block(LAGS, LAGS), block(LAGS, LAGS), block(2, PANEL, LAGS), block(2, PANEL, LAGS),
             block(*half), block(4, *half), block(8, *half), block(2, *half), block(4, 2 * width, SEG_LEN),
-            block(32, 8, 128), block(32, 8, 128), block(8, 32, 128), block(8, 128), block(8, 8, 128), block(4, 8, 128),
+            block(LAGS, 1, 128), block(1, 128), block(32, 1, 128),
             dma((2,)), dma((63,)), dma((1,)), dma((2,)), dma((31,)), dma((31,)),
             dma((2,)), dma((3,)), dma((3,)), dma((7,)), dma((7,)), dma((2,)),
-            dma((31,)), dma((31,)), dma((7,)), dma((7,)), dma((7,)), dma((7,)), dma((3,)), dma((3,)), dma((7,)), dma((7,)),
+            dma((255,)), dma((255,)), dma((31,)), dma((31,)), dma((7,)), dma((7,)),
         ],
         compiler_params=pltpu.CompilerParams(collective_id=0, has_side_effects=True, vmem_limit_bytes=24 * 2**20),
         name="cancel",
@@ -643,8 +638,7 @@
 
 def doppler_tables(shards, segments):
     short = DOPP // segments
-    order = np.arange(shards).reshape(-1, 2).T.reshape(-1)
-    angle = 2.0 * np.pi / short * (np.outer(order, np.arange(short)) % short)
+    angle = 2.0 * np.pi / short * (np.outer(np.arange(shards), np.arange(short)) % short)
     table = np.concatenate([np.cos(angle), np.sin(angle)], axis=1)
     turn = 2.0 * np.pi / DOPP * np.outer(np.arange(segments), np.arange(DOPP))
     turns = np.stack([np.cos(turn), np.sin(turn)])
@@ -652,8 +646,9 @@
 
 
 def doppler_kernel(samples, weights, cells, energies, table, turns, out, kept):
-    near, _, lanes = cells.shape
-    groups = near // 2
+    lanes = cells.shape[2]
+    groups = energies.shape[0] // 2
+    shards = cells.shape[0] // groups
     segments = turns.shape[1]
     width = lanes // segments // 2
     basis = halves(table[...])
@@ -662,7 +657,7 @@
         power = (energies[g] + energies[groups + g]) / samples
         scale = lax.rsqrt(samples * (power + EPSILON))
         by = jnp.broadcast_to(scale[0:1], (128, 128)).T[:width, 0:1]
-        rows = jnp.concatenate([cells[g], cells[groups + g]], axis=0)
+        rows = cells[shards * g : shards * g + shards, 0, :]
         wave = dot3(halves(rows.T), basis)
         total_r = total_i = None
         for s in range(segments):
@@ -694,10 +689,10 @@
 
 def doppler(weights, cells, energies, segments, samples):
     vmem = pl.BlockSpec(memory_space=pltpu.VMEM)
-    shards = 2 * cells.shape[1]
+    groups = energies.shape[0] // 2
+    shards = cells.shape[0] // groups
     table, turns = doppler_tables(shards, segments)
     width = cells.shape[2] // segments // 2
-    groups = cells.shape[0] // 2
     return pl.pallas_call(
         functools.partial(doppler_kernel, samples),
         out_shape=[

time: 60.1 us -> 69.2 us (1.15)
  the two profiles are of different devices: /device:TPU:1 before, /device:TPU:17 now
where the time goes in v6:
time: 69.2 us; the launch traced here: 69 us
  Pallas kernels  66.1 us (96%)
  local copies, waits for them, and re-layouts  1.67 us (2%)
  between operations  1.31 us (2%)
    pallas_call x1, Pallas kernels, cancel(): pl.pallas_call(cancel_kernel, out_shape=[jax.ShapeDtypeStruct((2 * width,...  64.5 us
    unnamed x8, local copies, waits for them, and re-layouts  1.67 us
    pallas_call x1, Pallas kernels, doppler(): pl.pallas_call(functools.partial(doppler_kernel, samples), out_shape=[jax...  1.58 us

profile of v6, /device:TPU:17, one launch (start us, length us, event | category | flops | bytes accessed | tf_op | source)
XLA Modules:
  0.0 69.0 jit_solution(16264732404490262410)
XLA Ops:
  1.3 0.0 copy-start
  1.3 0.9 %copy-done = f32[2,16,2048]{2,1,0:T(8,128)S(1)} copy-done((f32[2,16,2048]{2,1,0:T(8,128)S(1)}, f32[2,16,2048]{2,1,0:T(8,128)}, u32[]{:S(2)}) %copy-start) | copy-done | bytes 262168
  2.2 0.0 copy-start.3
  2.2 0.7 %copy-done.3 = f32[2,2048]{1,0:T(2,128)S(1)} copy-done((f32[2,2048]{1,0:T(2,128)S(1)}, f32[2,2048]{1,0:T(2,128)}, u32[]{:S(2)}) %copy-start.3) | copy-done | bytes 16408
  2.9 0.0 copy-start.1
  2.9 0.0 copy-start.2
  2.9 64.5 %cancel.1 = (f32[32,256]{1,0:T(8,128)S(1)}, f32[256,1,128]{2,1,0:T(1,128)S(1)}, f32[8,1,128]{2,1,0:T(1,128)S(1)}) custom-call(f32[1]{0:T(128)S(6)} %copy.7.loading, f32[2,2048]{1,0:T(2,128)S(1)} %copy-done.3, f32[2,16,2048]{2,1,0:T(8,128)S(1)} %copy-done), custom_call_target="tpu_custom_call" | custom-call | tf_op jit(solution)/shard_map/cancel/pallas_call | solution.py:615
  67.4 0.0 copy-done.1
  67.4 0.0 copy-done.2
  67.5 1.6 %doppler.1 = (f32[1,2,64,1024]{3,2,1,0:T(8,128)}, f32[32,256]{1,0:T(8,128)}) custom-call(f32[32,256]{1,0:T(8,128)S(1)} %get-tuple-element.7.weights, f32[256,1,128]{2,1,0:T(1,128)S(1)} %get-tuple-element.8.cells, f32[8,1,128]{2,1,0:T(1,128)S(1)} %get-tuple-element.9.energies, f32[64,512]{1,0:T(8,128)S(1)} %copy-done.1, f32[2,4,1024]{2,1,0:T(4,128)S(1)} %copy-done.2), custom_call_target="tpu_custom_call" | custom-call | tf_op jit(solution)/shard_map/doppler/pallas_call | solution.py:696
Async XLA Ops:
  1.3 1.0 %copy-start = (f32[2,16,2048]{2,1,0:T(8,128)S(1)}, f32[2,16,2048]{2,1,0:T(8,128)}, u32[]{:S(2)}) copy-start(f32[2,16,2048]{2,1,0:T(8,128)} %surveillance.1) | copy-start | bytes 786436
  2.2 0.7 %copy-start.3 = (f32[2,2048]{1,0:T(2,128)S(1)}, f32[2,2048]{1,0:T(2,128)}, u32[]{:S(2)}) copy-start(f32[2,2048]{1,0:T(2,128)} %reference.1) | copy-start | bytes 49156
  2.9 64.5 %copy-start.1 = (f32[64,512]{1,0:T(8,128)S(1)}, f32[64,512]{1,0:T(8,128)}, u32[]{:S(2)}) copy-start(f32[64,512]{1,0:T(8,128)} %constant.4.clone.table) | copy-start | bytes 393220
  2.9 64.5 %copy-start.2 = (f32[2,4,1024]{2,1,0:T(4,128)S(1)}, f32[2,4,1024]{2,1,0:T(4,128)}, u32[]{:S(2)}) copy-start(f32[2,4,1024]{2,1,0:T(4,128)} %constant.5.clone.turns) | copy-start | bytes 98308

commit v7 on v5

--- a/solution.py
+++ b/solution.py
@@ -366,8 +366,8 @@
 
 
 def cancel_kernel(
-    loading, reference_hbm, surveillance_hbm, weights, cells, energies,
-    reference, surveillance, fetch_sem, table, halo, tail, mine, gram_pair, gram_all, real, imag, top, done,
+    loading, reference, surveillance_hbm, weights, cells, energies,
+    surveillance, fetch_sem, table, halo, tail, mine, gram_pair, gram_all, real, imag, top, done,
     pair, ring_y, ring_z, cross, residual, corr, landed, turned, power, power_z, power_y,
     edge_sem, tail_send, tail_recv, gram_sem, gram_send, gram_recv,
     pair_sem, y_send, y_recv, z_send, z_recv, out_sem,
@@ -378,14 +378,11 @@
     count = lax.axis_size(TM)
     here = place(TM)
     core, y, z, far, near = place(PAIR), place(ALONG_Y), place(ALONG_Z), place(FAR), place(NEAR)
-    fetch_r = pltpu.make_async_copy(reference_hbm, reference, fetch_sem.at[0])
-    fetch_r.start()
-    fetch_s = pltpu.make_async_copy(surveillance_hbm, surveillance, fetch_sem.at[1])
-    fetch_s.start()
+    fetch = pltpu.make_async_copy(surveillance_hbm, surveillance, fetch_sem.at[0])
+    fetch.start()
     barrier = pltpu.get_barrier_semaphore()
     total = greet(barrier, TM)
     total += greet(barrier, NEAR, 4)
-    fetch_r.wait()
 
     def fill(tile, windows):
         delayed = [toeplitz(x, 128)[:, 128:] for x in windows]
@@ -463,7 +460,7 @@
     gram_all[far] = gram_pair[0] + gram_pair[1]
     to_gram = Exchange(FAR, lambda p: gram_all.at[far], lambda p: gram_all.at[p], gram_send, gram_recv).start()
 
-    fetch_s.wait()
+    fetch.wait()
     segments = length // SEG_LEN
 
     def taps_of(segment):
@@ -627,10 +624,10 @@
             jax.ShapeDtypeStruct((8, 32, 128), jnp.float32),
             jax.ShapeDtypeStruct((8, 8, 128), jnp.float32),
         ],
-        in_specs=[pl.BlockSpec(memory_space=pltpu.SMEM)] + [pl.BlockSpec(memory_space=pltpu.HBM)] * 2,
+        in_specs=[pl.BlockSpec(memory_space=pltpu.SMEM), vmem, pl.BlockSpec(memory_space=pltpu.HBM)],
         out_specs=[vmem] * 3,
         scratch_shapes=[
-            block(*reference.shape), block(*surveillance.shape), dma((2,)),
+            block(*surveillance.shape), dma((1,)),
             pltpu.VMEM((2, 2, 128, LAGS + length), jnp.bfloat16),
             block(2, LAGS), block(2, LAGS), block(2, *half), block(2, 4, 128), block(32, 4, 128),
             block(LAGS, LAGS), block(LAGS, LAGS), block(2, PANEL, LAGS), block(2, PANEL, LAGS),
@@ -640,7 +637,7 @@
             dma((2,)), dma((3,)), dma((3,)), dma((7,)), dma((7,)), dma((2,)),
             dma((31,)), dma((31,)), dma((7,)), dma((7,)), dma((7,)), dma((7,)), dma((3,)), dma((3,)), dma((7,)), dma((7,)),
         ],
-        compiler_params=pltpu.CompilerParams(collective_id=0, has_side_effects=True, vmem_limit_bytes=24 * 2**20),
+        compiler_params=pltpu.CompilerParams(collective_id=0, has_side_effects=True, vmem_limit_bytes=56200000),
         name="cancel",
     )(loading, reference, surveillance)
 

time: 60.3 us -> 59.2 us (0.982)
  local copies, waits for them, and re-layouts: 1.67 us -> 0.72 us
    unnamed x8 -> x6, local copies, waits for them, and re-layouts: 1.67 us -> 0.72 us
where the time goes in v7:
time: 59.2 us; the launch traced here: 59 us
  Pallas kernels  57 us (96%)
  between operations  1.31 us (2%)
  local copies, waits for them, and re-layouts  0.72 us (1%)
    pallas_call x1, Pallas kernels, cancel(): pl.pallas_call(cancel_kernel, out_shape=[jax.ShapeDtypeStruct((2 * width,...  55.4 us
    pallas_call x1, Pallas kernels, doppler(): pl.pallas_call(functools.partial(doppler_kernel, samples), out_shape=[jax...  1.57 us

profile of v7, /device:TPU:1, one launch (start us, length us, event | category | flops | bytes accessed | tf_op | source)
XLA Modules:
  0.0 59.0 jit_solution(17805041734905031455)
XLA Ops:
  1.3 0.0 copy-start.2
  1.3 0.7 %copy-done.2 = f32[2,2048]{1,0:T(2,128)S(1)} copy-done((f32[2,2048]{1,0:T(2,128)S(1)}, f32[2,2048]{1,0:T(2,128)}, u32[]{:S(2)}) %copy-start.2) | copy-done | bytes 16408
  2.0 0.0 copy-start
  2.0 0.0 copy-start.1
  2.0 55.4 %cancel.1 = (f32[32,256]{1,0:T(8,128)S(1)}, f32[8,32,128]{2,1,0:T(8,128)S(1)}, f32[8,8,128]{2,1,0:T(8,128)S(1)}) custom-call(f32[1]{0:T(128)S(6)} %copy.7.loading, f32[2,2048]{1,0:T(2,128)S(1)} %copy-done.2, f32[2,16,2048]{2,1,0:T(8,128)} %surveillance_hbm.1), custom_call_target="tpu_custom_call" | custom-call | tf_op jit(solution)/shard_map/cancel/pallas_call | solution.py:620
  57.5 0.0 copy-done
  57.5 0.0 copy-done.1
  57.5 1.6 %doppler.1 = (f32[1,2,64,1024]{3,2,1,0:T(8,128)}, f32[32,256]{1,0:T(8,128)}) custom-call(f32[32,256]{1,0:T(8,128)S(1)} %get-tuple-element.7.weights, f32[8,32,128]{2,1,0:T(8,128)S(1)} %get-tuple-element.8.cells, f32[8,8,128]{2,1,0:T(8,128)S(1)} %get-tuple-element.9.energies, f32[64,512]{1,0:T(8,128)S(1)} %copy-done, f32[2,4,1024]{2,1,0:T(4,128)S(1)} %copy-done.1), custom_call_target="tpu_custom_call" | custom-call | tf_op jit(solution)/shard_map/doppler/pallas_call | solution.py:702
Async XLA Ops:
  1.3 0.7 %copy-start.2 = (f32[2,2048]{1,0:T(2,128)S(1)}, f32[2,2048]{1,0:T(2,128)}, u32[]{:S(2)}) copy-start(f32[2,2048]{1,0:T(2,128)} %reference.1) | copy-start | bytes 49156
  2.0 55.5 %copy-start = (f32[64,512]{1,0:T(8,128)S(1)}, f32[64,512]{1,0:T(8,128)}, u32[]{:S(2)}) copy-start(f32[64,512]{1,0:T(8,128)} %constant.4.clone.table) | copy-start | bytes 393220
  2.0 55.5 %copy-start.1 = (f32[2,4,1024]{2,1,0:T(4,128)S(1)}, f32[2,4,1024]{2,1,0:T(4,128)}, u32[]{:S(2)}) copy-start(f32[2,4,1024]{2,1,0:T(4,128)} %constant.5.clone.turns) | copy-start | bytes 98308

commit v8 on v7

--- a/solution.py
+++ b/solution.py
@@ -67,14 +67,19 @@
         lax.fori_loop(1, count, lambda d, carry: (act(d), carry)[1], 0)
 
 
+def wrapped(index, count):
+    return jnp.where(index >= count, index - count, index)
+
+
 class Exchange:
     def __init__(self, axes, src, dst, send, recv):
         self.axes, self.src, self.dst, self.send, self.recv = axes, src, dst, send, recv
         self.count = int(np.prod([lax.axis_size(a) for a in axes]))
 
-    def copy(self, d):
+    def copy(self, d, there=None):
         here = place(self.axes)
-        there = lax.rem(here + d, self.count)
+        if there is None:
+            there = wrapped(here + d, self.count)
         return pltpu.make_async_remote_copy(
             src_ref=self.src(there),
             dst_ref=self.dst(here),
@@ -89,7 +94,8 @@
         return self
 
     def wait(self):
-        each(self.count, lambda d: self.copy(d).wait())
+        partner = wrapped(place(self.axes) + 1, self.count)
+        each(self.count, lambda d: self.copy(d, partner).wait())
 
 
 def place(axes):
@@ -113,7 +119,7 @@
 
     def one(d):
         pl.semaphore_signal(
-            barrier, inc=1, device_id=device(axes, lax.rem(here + d, count)), device_id_type=MESH
+            barrier, inc=1, device_id=device(axes, wrapped(here + d, count)), device_id_type=MESH
         )
 
     if skip:

time: 59.2 us -> 59 us (level)
  no operation moved by 1% of the time
where the time goes in v8:
time: 59 us; the launch traced here: 58.9 us
  Pallas kernels  56.9 us (96%)
  between operations  1.31 us (2%)
  local copies, waits for them, and re-layouts  0.72 us (1%)
    pallas_call x1, Pallas kernels, cancel(): pl.pallas_call(cancel_kernel, out_shape=[jax.ShapeDtypeStruct((2 * width,...  55.3 us
    pallas_call x1, Pallas kernels, doppler(): pl.pallas_call(functools.partial(doppler_kernel, samples), out_shape=[jax...  1.57 us

profile of v8, /device:TPU:1, one launch (start us, length us, event | category | flops | bytes accessed | tf_op | source)
XLA Modules:
  0.0 58.9 jit_solution(467555246041272837)
XLA Ops:
  1.3 0.0 copy-start.2
  1.3 0.7 %copy-done.2 = f32[2,2048]{1,0:T(2,128)S(1)} copy-done((f32[2,2048]{1,0:T(2,128)S(1)}, f32[2,2048]{1,0:T(2,128)}, u32[]{:S(2)}) %copy-start.2) | copy-done | bytes 16408
  2.0 0.0 copy-start
  2.0 0.0 copy-start.1
  2.0 55.3 %cancel.1 = (f32[32,256]{1,0:T(8,128)S(1)}, f32[8,32,128]{2,1,0:T(8,128)S(1)}, f32[8,8,128]{2,1,0:T(8,128)S(1)}) custom-call(f32[1]{0:T(128)S(6)} %copy.7.loading, f32[2,2048]{1,0:T(2,128)S(1)} %copy-done.2, f32[2,16,2048]{2,1,0:T(8,128)} %surveillance_hbm.1), custom_call_target="tpu_custom_call" | custom-call | tf_op jit(solution)/shard_map/cancel/pallas_call | solution.py:626
  57.3 0.0 copy-done
  57.3 0.0 copy-done.1
  57.3 1.6 %doppler.1 = (f32[1,2,64,1024]{3,2,1,0:T(8,128)}, f32[32,256]{1,0:T(8,128)}) custom-call(f32[32,256]{1,0:T(8,128)S(1)} %get-tuple-element.7.weights, f32[8,32,128]{2,1,0:T(8,128)S(1)} %get-tuple-element.8.cells, f32[8,8,128]{2,1,0:T(8,128)S(1)} %get-tuple-element.9.energies, f32[64,512]{1,0:T(8,128)S(1)} %copy-done, f32[2,4,1024]{2,1,0:T(4,128)S(1)} %copy-done.1), custom_call_target="tpu_custom_call" | custom-call | tf_op jit(solution)/shard_map/doppler/pallas_call | solution.py:708
Async XLA Ops:
  1.3 0.7 %copy-start.2 = (f32[2,2048]{1,0:T(2,128)S(1)}, f32[2,2048]{1,0:T(2,128)}, u32[]{:S(2)}) copy-start(f32[2,2048]{1,0:T(2,128)} %reference.1) | copy-start | bytes 49156
  2.0 55.3 %copy-start = (f32[64,512]{1,0:T(8,128)S(1)}, f32[64,512]{1,0:T(8,128)}, u32[]{:S(2)}) copy-start(f32[64,512]{1,0:T(8,128)} %constant.4.clone.table) | copy-start | bytes 393220
  2.0 55.3 %copy-start.1 = (f32[2,4,1024]{2,1,0:T(4,128)S(1)}, f32[2,4,1024]{2,1,0:T(4,128)}, u32[]{:S(2)}) copy-start(f32[2,4,1024]{2,1,0:T(4,128)} %constant.5.clone.turns) | copy-start | bytes 98308

commit v9 on v7

--- a/solution.py
+++ b/solution.py
@@ -349,7 +349,9 @@
     i0 = lax.broadcasted_iota(jnp.int32, (LAGS, LAGS), 0)
     i1 = lax.broadcasted_iota(jnp.int32, (LAGS, LAGS), 1)
     flip = jnp.where(i0 + i1 == LAGS - 1, 1.0, 0.0)
-    behind = pltpu.roll(dot(column, flip), 1, 1)
+    flip = flip.astype(jnp.bfloat16)
+    turned = [lax.dot_general(x, flip, NN, preferred_element_type=jnp.float32) for x in thirds(column)]
+    behind = pltpu.roll(turned[0] + (turned[1] + turned[2]), 1, 1)
     lane = lax.broadcasted_iota(jnp.int32, behind.shape, 1)
     behind = jnp.where(lane == 0, 0.0, behind)
     base_r = toeplitz(jnp.concatenate([column[0:1], behind[0:1]], axis=1), LAGS)[:, :LAGS]

time: 59.2 us -> 59.4 us (level)
  no operation moved by 1% of the time
where the time goes in v9:
time: 59.4 us; the launch traced here: 59.2 us
  Pallas kernels  57.2 us (96%)
  between operations  1.31 us (2%)
  local copies, waits for them, and re-layouts  0.72 us (1%)
    pallas_call x1, Pallas kernels, cancel(): pl.pallas_call(cancel_kernel, out_shape=[jax.ShapeDtypeStruct((2 * width,...  55.6 us
    pallas_call x1, Pallas kernels, doppler(): pl.pallas_call(functools.partial(doppler_kernel, samples), out_shape=[jax...  1.57 us

profile of v9, /device:TPU:1, one launch (start us, length us, event | category | flops | bytes accessed | tf_op | source)
XLA Modules:
  0.0 59.2 jit_solution(14752133886614025192)
XLA Ops:
  1.3 0.0 copy-start.2
  1.3 0.7 %copy-done.2 = f32[2,2048]{1,0:T(2,128)S(1)} copy-done((f32[2,2048]{1,0:T(2,128)S(1)}, f32[2,2048]{1,0:T(2,128)}, u32[]{:S(2)}) %copy-start.2) | copy-done | bytes 16408
  2.0 0.0 copy-start
  2.0 0.0 copy-start.1
  2.0 55.6 %cancel.1 = (f32[32,256]{1,0:T(8,128)S(1)}, f32[8,32,128]{2,1,0:T(8,128)S(1)}, f32[8,8,128]{2,1,0:T(8,128)S(1)}) custom-call(f32[1]{0:T(128)S(6)} %copy.7.loading, f32[2,2048]{1,0:T(2,128)S(1)} %copy-done.2, f32[2,16,2048]{2,1,0:T(8,128)} %surveillance_hbm.1), custom_call_target="tpu_custom_call" | custom-call | tf_op jit(solution)/shard_map/cancel/pallas_call | solution.py:622
  57.6 0.0 copy-done
  57.6 0.0 copy-done.1
  57.6 1.6 %doppler.1 = (f32[1,2,64,1024]{3,2,1,0:T(8,128)}, f32[32,256]{1,0:T(8,128)}) custom-call(f32[32,256]{1,0:T(8,128)S(1)} %get-tuple-element.7.weights, f32[8,32,128]{2,1,0:T(8,128)S(1)} %get-tuple-element.8.cells, f32[8,8,128]{2,1,0:T(8,128)S(1)} %get-tuple-element.9.energies, f32[64,512]{1,0:T(8,128)S(1)} %copy-done, f32[2,4,1024]{2,1,0:T(4,128)S(1)} %copy-done.1), custom_call_target="tpu_custom_call" | custom-call | tf_op jit(solution)/shard_map/doppler/pallas_call | solution.py:704
Async XLA Ops:
  1.3 0.7 %copy-start.2 = (f32[2,2048]{1,0:T(2,128)S(1)}, f32[2,2048]{1,0:T(2,128)}, u32[]{:S(2)}) copy-start(f32[2,2048]{1,0:T(2,128)} %reference.1) | copy-start | bytes 49156
  2.0 55.6 %copy-start = (f32[64,512]{1,0:T(8,128)S(1)}, f32[64,512]{1,0:T(8,128)}, u32[]{:S(2)}) copy-start(f32[64,512]{1,0:T(8,128)} %constant.4.clone.table) | copy-start | bytes 393220
  2.0 55.6 %copy-start.1 = (f32[2,4,1024]{2,1,0:T(4,128)S(1)}, f32[2,4,1024]{2,1,0:T(4,128)}, u32[]{:S(2)}) copy-start(f32[2,4,1024]{2,1,0:T(4,128)} %constant.5.clone.turns) | copy-start | bytes 98308
